TPU v7x, 32 devices: a whole 2x2x4 slice. The times are simulated.
32 devices in a mesh: gx: 8 (over z, x), gy: 4 (over y, core).
Axes of the slice: x: 2, y: 2, z: 4, core: 2. Of those that a mesh axis runs over, the one named last changes fastest.
Arguments:
- potential_warmth: float32 [576, 30, 3000], P(('gx', 'gy')), may hold values from -6 to 6
- saltiness_anomaly: float32 [576, 30, 3000], P(('gx', 'gy')), may hold values from -6 to 6
- topmost_thermal_inflow: float32 [576, 3000], P(('gx', 'gy')), may hold values from -8 to 8
- diffusivity_factor: float32 [29], replicated, may hold values from 0.05 to 5
- place_tile_number: int32 [576], P(('gx', 'gy')), may hold values from -1 to 575, as said below
- place_stack_strata: int32 [576, 3000], P(('gx', 'gy')), may hold values from 0 to 30, as said below
- mesh_stack_strata: int32 [1200, 1440], P('gy', 'gx'), may hold values from 0 to 30, as said below
Outputs:
- temperature_new: float32 [576, 30, 3000], P(('gx', 'gy'))
- salinity_new: float32 [576, 30, 3000], P(('gx', 'gy'))
- surface_height: float32 [1200, 1440], P('gy', 'gx')
- misfit_vector: float32 [1200, 1440], P('gy', 'gx')
Inputs may be any that keep to these rules, and one draw needn't show every extreme that they name: `place_tile_number`: block (by, bx) has id by * 24 + bx. Every block holding an ocean column (mesh_stack_strata > 0) sits in exactly one slot, no block twice, and unlisted blocks are all land. The device at gx, gy holds only blocks with by // 6 = gy, and at most 3 blocks with the same bx // 3; some device holds exactly 3 such blocks. `place_stack_strata`: entry i * 60 + j of a slot equals mesh_stack_strata at row by * 50 + i, column bx * 60 + j of the slot's block; empty slots hold zeros. `mesh_stack_strata`: zero on land.
All inputs are finite; a program needn't handle non-finite values.
Results may differ from a plain program's by a relative error of at most 0.0003.
Values sent between devices are 32-bit elements; how exact they have to be, the bound alone decides.
No kernel may reach another device: no remote copies, remote signals or barrier semaphores. Data moves between devices by JAX's collectives and lax.ppermute only.
A program may use at most 256 MiB of HBM per device.

v0:
```python
import jax
import jax.numpy as jnp
from jax import lax
from jax.sharding import PartitionSpec as P

TILE_SPAN_EASTWARD = 60
TILE_SPAN_NORTH = 50
KX = 3
KY = 6
SEA_DEPTH_STRATA = 30
ITERS = 3


HALINE_CONTRACT = 0.8
THERMAL_EXPANSE = 0.6
DAMPING = 0.05


def swapped(value, axis, bit):
    mask = 2**bit
    pairs = [(source, source ^ mask) for source in range(lax.axis_size(axis))]
    return lax.ppermute(value, axis, pairs)


def with_halo(cells, sides, width):
    for axis, dim in sides:
        count = lax.axis_size(axis)
        head = lax.slice_in_dim(cells, 0, width, axis=dim)
        tail = lax.slice_in_dim(cells, cells.shape[dim] - width, cells.shape[dim], axis=dim)
        cells = jnp.concatenate(
            [
                lax.ppermute(tail, axis, [(i, (i + 1) % count) for i in range(count)]),
                cells,
                lax.ppermute(head, axis, [((i + 1) % count, i) for i in range(count)]),
            ],
            axis=dim,
        )
    return cells


def thomas_vertical_inverse(
    potential_warmth,
    saltiness_anomaly,
    topmost_thermal_inflow,
    diffusivity_factor,
    marine_strata_number,
):
    wet_strata_number = potential_warmth.shape[1]
    coupling = [
        jnp.where(
            stratum_position + 1 < marine_strata_number, diffusivity_factor[stratum_position], 0.0
        )
        for stratum_position in range(wet_strata_number - 1)
    ]
    forced = jnp.where(marine_strata_number > 0, topmost_thermal_inflow, 0.0)
    gains = []
    heat_rows = []
    salt_rows = []
    for stratum_position in range(wet_strata_number):
        pivots = jnp.ones(topmost_thermal_inflow.shape, jnp.float32)
        thermal_forcing_part = potential_warmth[:, stratum_position, :]
        salt_term = saltiness_anomaly[:, stratum_position, :]
        if stratum_position == 0:
            thermal_forcing_part = thermal_forcing_part + forced
        if stratum_position + 1 < wet_strata_number:
            pivots = pivots + coupling[stratum_position]
        if stratum_position > 0:
            pivots = (
                pivots
                + coupling[stratum_position - 1]
                - coupling[stratum_position - 1] * gains[stratum_position - 1]
            )
            thermal_forcing_part = (
                thermal_forcing_part
                + coupling[stratum_position - 1] * heat_rows[stratum_position - 1]
            )
            salt_term = salt_term + coupling[stratum_position - 1] * salt_rows[stratum_position - 1]
        if stratum_position + 1 < wet_strata_number:
            gains.append(coupling[stratum_position] / pivots)
        else:
            gains.append(jnp.zeros_like(pivots))
        heat_rows.append(thermal_forcing_part / pivots)
        salt_rows.append(salt_term / pivots)
    heat_out = [heat_rows[wet_strata_number - 1]]
    salt_out = [salt_rows[wet_strata_number - 1]]
    for stratum_position in range(wet_strata_number - 2, -1, -1):
        heat_out.append(heat_rows[stratum_position] + gains[stratum_position] * heat_out[-1])
        salt_out.append(salt_rows[stratum_position] + gains[stratum_position] * salt_out[-1])
    return (jnp.stack(heat_out[::-1], axis=1), jnp.stack(salt_out[::-1], axis=1))


def weight_balanced(revised_warmth, revised_saltiness, marine_strata_number):
    running = jnp.zeros(marine_strata_number.shape, jnp.float32)
    layers_out = []
    for stratum_position in range(revised_warmth.shape[1]):
        mass_per_volume = jnp.where(
            stratum_position < marine_strata_number,
            HALINE_CONTRACT * revised_saltiness[:, stratum_position, :]
            - THERMAL_EXPANSE * revised_warmth[:, stratum_position, :],
            0.0,
        )
        running = running + mass_per_volume
        layers_out.append(running)
    return jnp.stack(layers_out, axis=1)


def locate(keys, wanted):
    matches = keys[None, :] == wanted[:, None]
    indices = jnp.arange(keys.shape[0], dtype=jnp.int32)
    return (jnp.sum(jnp.where(matches, indices[None, :], 0), axis=1), jnp.any(matches, axis=1))


def to_region(blocks):
    wet_strata_number = blocks.shape[1]
    shaped = blocks.reshape(
        KY, KX, wet_strata_number, TILE_SPAN_NORTH, TILE_SPAN_EASTWARD
    ).transpose(2, 0, 3, 1, 4)
    return shaped.reshape(wet_strata_number, KY * TILE_SPAN_NORTH, KX * TILE_SPAN_EASTWARD)


def fold_rows(rows):
    partner = rows
    for bit_index in range(lax.axis_size("gx").bit_length() - 1):
        partner = swapped(partner, "gx", bit_index)
    return partner[:, ::-1]


def sides(field, padded, folded, index_y, span_y):
    east_side = padded[:, 1:-1, 2:]
    west_side = padded[:, 1:-1, :-2]
    north_row = jnp.where(index_y == span_y - 1, folded, padded[:, -1, 1:-1])
    south_row = jnp.where(index_y == 0, 0.0, padded[:, 0, 1:-1])
    north_side = jnp.concatenate([field[:, 1:, :], north_row[:, None, :]], axis=1)
    south_side = jnp.concatenate([south_row[:, None, :], field[:, :-1, :]], axis=1)
    return (east_side, west_side, north_side, south_side)


def global_sum(values):
    return lax.psum(jnp.sum(values), ("gx", "gy"))


def on_device(
    potential_warmth,
    saltiness_anomaly,
    topmost_thermal_inflow,
    diffusivity_factor,
    place_tile_number,
    place_stack_strata,
    mesh_stack_strata,
):
    revised_warmth, revised_saltiness = thomas_vertical_inverse(
        potential_warmth,
        saltiness_anomaly,
        topmost_thermal_inflow,
        diffusivity_factor,
        place_stack_strata,
    )
    normal_stress = weight_balanced(revised_warmth, revised_saltiness, place_stack_strata)
    span_x = lax.axis_size("gx")
    span_y = lax.axis_size("gy")
    index_x = lax.axis_index("gx")
    index_y = lax.axis_index("gy")
    capacity = (KX * KY + span_x - 1) // span_x
    blocks_x = KX * span_x
    slot_count = place_tile_number.shape[0]
    rows_out = span_x * capacity
    valid = place_tile_number >= 0
    owner_x = jnp.where(valid, jnp.maximum(place_tile_number, 0) % blocks_x // KX, -1)
    slot_order = jnp.arange(slot_count)
    earlier = (owner_x[None, :] == owner_x[:, None]) & (slot_order[None, :] < slot_order[:, None])
    ranking = jnp.sum(earlier.astype(jnp.int32), axis=1)
    send_row = jnp.where(valid, owner_x * capacity + ranking, -1)
    source, filled = locate(send_row, jnp.arange(rows_out, dtype=jnp.int32))
    send_ids = jnp.where(filled, place_tile_number[source], -1)
    wanted = (index_y * KY + slot_order // KX) * blocks_x + index_x * KX + slot_order % KX
    region_rows = mesh_stack_strata.shape[0]
    region_cols = mesh_stack_strata.shape[1]
    send_cols = jnp.where(filled[:, None, None], jnp.take(normal_stress, source, axis=0), 0.0)
    got_cols, got_ids = (
        lax.all_to_all(send_cols, "gx", split_axis=0, concat_axis=0, tiled=True),
        lax.all_to_all(send_ids, "gx", split_axis=0, concat_axis=0, tiled=True),
    )
    spots, found = locate(got_ids, wanted)
    placed = jnp.where(found[:, None, None], jnp.take(got_cols, spots, axis=0), 0.0)
    region = to_region(placed)
    partial_value = jnp.zeros((region_rows, region_cols), jnp.float32)
    boundary = (1.0, 1.0, 1.0, 1.0)
    depth = mesh_stack_strata.astype(jnp.float32)
    stacked = jnp.concatenate([region, depth[None]], axis=0)
    folded_top = fold_rows(stacked[:, -1, :])
    padded = with_halo(stacked, (("gy", 1), ("gx", 2)), 1)
    beside_all = sides(stacked, padded, folded_top, index_y, span_y)
    layer_index = jnp.arange(SEA_DEPTH_STRATA, dtype=jnp.float32)[:, None, None]
    rhs = partial_value
    weights = []
    for neighbour, edge_mask in zip(beside_all, boundary):
        face_levels = jnp.minimum(depth, neighbour[-1])
        face_flux = jnp.sum(
            jnp.where(layer_index < face_levels, neighbour[:-1] - region, 0.0), axis=0
        )
        rhs = rhs + face_flux * edge_mask
        weights.append(face_levels / SEA_DEPTH_STRATA)
    rhs = rhs / SEA_DEPTH_STRATA
    damping = jnp.where(depth > 0, DAMPING, 1.0)
    diagonal = damping + weights[0] + weights[1] + weights[2] + weights[3]
    elevation = jnp.zeros((region_rows, region_cols), jnp.float32)
    misfit_vector = rhs
    precond = misfit_vector / diagonal
    direction = precond
    precond_dot = global_sum(misfit_vector * precond)
    for iteration in range(ITERS):
        field_pad = with_halo(direction[None], (("gy", 1), ("gx", 2)), 1)
        field_fold = fold_rows(direction[-1:, :])
        result = damping * direction
        for operate_neighbour, weight in zip(
            sides(direction[None], field_pad, field_fold, index_y, span_y), weights
        ):
            result = result + weight * (direction - operate_neighbour[0])
        step_size = precond_dot / lax.psum(jnp.sum(direction * result), ("gx", "gy"))
        elevation = elevation + step_size * direction
        misfit_vector = misfit_vector - step_size * result
        precond = misfit_vector / diagonal
        next_dot = global_sum(misfit_vector * precond)
        direction = precond + next_dot / precond_dot * direction
        precond_dot = next_dot
    return (revised_warmth, revised_saltiness, elevation, misfit_vector)


def solution(mesh):
    in_specs = (
        P(("gx", "gy"), None, None),
        P(("gx", "gy"), None, None),
        P(("gx", "gy"), None),
        P(),
        P(("gx", "gy")),
        P(("gx", "gy"), None),
        P("gy", "gx"),
    )
    out_specs = (
        P(("gx", "gy"), None, None),
        P(("gx", "gy"), None, None),
        P("gy", "gx"),
        P("gy", "gx"),
    )
    return jax.shard_map(
        on_device, mesh=mesh, in_specs=in_specs, out_specs=out_specs, check_vma=False
    )
```

profile of v0, /device:TPU:0, one launch (start us, length us, event | category | flops | bytes accessed | tf_op | source)
XLA Modules:
  0.0 878.8 jit_solution(5370469227735463066)
XLA Ops:
  5.0 7.3 all-to-all-start
  12.3 10.2 %fusion.305 = (f32[18,1,3000]{2,1,0:T(1,128)S(1)}, f32[18,1,3000]{2,1,0:T(1,128)S(1)}, f32[18,1,3000]{2,1,0:T(1,128)S(1)}, f32[18,1,3000]{2,1,0:T(1,128)S(1)}, f...) fusion(f32[18,30,3000]{2,1,0:T(8,128)} %param.8), kind=kLoop, calls=%fused_computation.766 | loop fusion | bytes 4752000 | tf_op jit(solution)/shard_map/slice | solution.py:62
  22.5 15.6 %fusion.304 = (f32[18,1,3000]{2,1,0:T(1,128)}, f32[18,1,3000]{2,1,0:T(1,128)S(1)}, f32[18,1,3000]{2,1,0:T(1,128)S(1)}, f32[18,1,3000]{2,1,0:T(1,128)S(1)}, f32[1...) fusion(f32[18,30,3000]{2,1,0:T(8,128)} %param.8), kind=kLoop, calls=%fused_computation.765 | loop fusion | bytes 8208000 | tf_op jit(solution)/shard_map/slice | solution.py:62
  47.4 6.2 fusion.101
  54.3 6.1 fusion.98
  60.7 20.0 %fusion.206 = (f32[18,3000]{1,0:T(8,128)}, f32[18,3000]{1,0:T(8,128)}, f32[18,3000]{1,0:T(8,128)}, f32[18,3000]{1,0:T(8,128)}, f32[18,3000]{1,0:T(8,128)}, /*ind...) fusion(f32[18,1,3000]{2,1,0:T(1,128)S(1)} %get-tuple-element.25, ...), kind=kLoop, calls=%fused_computation.453 | loop fusion | flops 11070000 | bytes 13122092 | tf_op jit(solution)/shard_map/div | solution.py:83
  81.1 19.2 %fusion.203 = (f32[18,3000]{1,0:T(8,128)}, f32[18,3000]{1,0:T(8,128)}, f32[18,3000]{1,0:T(8,128)}, f32[18,3000]{1,0:T(8,128)}, f32[18,3000]{1,0:T(8,128)}, /*ind...) fusion(pred[18,3000]{1,0:T(8,128)(4,1)S(1)} %get-tuple-element., ...), kind=kLoop, calls=%fused_computation.450 | loop fusion | flops 9990000 | bytes 12906092 | tf_op jit(solution)/shard_map/div | solution.py:82
  100.5 32.8 %select_add_fusion.58 = (f32[18,3000]{1,0:T(8,128)}, f32[18,3000]{1,0:T(8,128)}, f32[18,3000]{1,0:T(8,128)S(1)}, f32[18,3000]{1,0:T(8,128)S(1)}, f32[18,3000]{1,...) fusion(f32[]{:T(128)} %bitcast.57, ...), kind=kLoop, calls=%fused_computation.580 | loop fusion | flops 21492000 | bytes 33804116 | tf_op jit(solution)/shard_map/add | solution.py:102
  193.7 34.0 %stack.371 = f32[18,30,3000]{2,1,0:T(8,128)} concatenate(f32[18,1,3000]{2,1,0:T(1,128)S(1)} %copy-done.89, f32[18,1,3000]{2,1,0:T(1,128)} %copy.368, f32[18,1,3000]{2,1,0:T(1,128)} %copy.369, f32[18,1,3000]{2,1,0:T(1,128)} %copy.370, f32[18,1,3000]{2,1,0:T(1,128)} %copy.371, f32[18,1,3000]{2,1,0:T(1,128)} %copy.372, f32[18,1,3000]{2,1,0:T(1,128)} %copy.373, ...), dimensions={1} | concatenate | bytes 12960000 | tf_op jit(solution)/shard_map/stack | solution.py:104
  227.7 7.7 gather_fusion.1
  235.4 9.5 %select_select_fusion = f32[24,30,3000]{2,1,0:T(8,128)} fusion(f32[24,30,3000]{2,1,0:T(8,128)} %gather_fusion.1, pred[24]{0:T(512)(128)(4,1)S(1)} %copy-done.114, pred[24]{0:T(512)(128)(4,1)S(1)} %copy-done.113), kind=kLoop, calls=%fused_computation.6 | loop fusion | flops 4320000 | bytes 17280048 | tf_op jit(solution)/shard_map/jit(_where)/select_n | solution.py:178
  245.6 6.1 all-to-all-start.1
  274.1 10.3 %copy.402 = f32[18,30,3000]{2,1,0:T(8,128)} copy(f32[18,30,3000]{2,0,1:T(8,128)} %get-tuple-element.284) | data formatting | bytes 12960000
  284.5 10.4 %copy.403 = f32[18,30,3000]{2,1,0:T(8,128)} copy(f32[18,30,3000]{2,0,1:T(8,128)} %get-tuple-element.283) | data formatting | bytes 12960000
  296.9 160.0 %all-to-all-done.1 = f32[24,30,3000]{2,1,0:T(8,128)} async-done(((f32[24,30,3000]{2,1,0:T(8,128)}), f32[24,30,3000]{2,1,0:T(8,128)}, u32[]{:S(2)}, u32[]{:S(2)}) %all-to-all-start.1) | async-done | bytes 8640032 | tf_op jit(solution)/shard_map/all_to_all | solution.py:180
  456.9 7.6 gather_fusion.2
  464.5 14.0 %gather.16 = f32[6,3,30,50,60]{4,3,2,1,0:T(8,128)} reshape(f32[18,30,3000]{2,1,0:T(8,128)} %gather_fusion.2) | data formatting | bytes 12960000 | tf_op jit(solution)/shard_map/jit(_take)/gather | solution.py:184
  478.5 13.4 %select_bitcast_fusion = f32[30,6,50,3,60]{4,2,0,3,1:T(8,128)} fusion(f32[6,3,30,50,60]{4,3,2,1,0:T(8,128)} %gather.16, pred[6,3]{1,0:T(8,128)(4,1)S(1)} %compare_and_fusion, pred[6,3]{1,0:T(8,128)(4,1)S(1)} %broadcast_in_dim.336), kind=kLoop, calls=%fused_computation.3 | loop fusion | flops 3240000 | bytes 12960036 | tf_op jit(solution)/shard_map/transpose | solution.py:117
  491.9 17.3 %copy.396 = f32[30,6,50,3,60]{4,3,2,1,0:T(4,128)} copy(f32[30,6,50,3,60]{4,2,0,3,1:T(8,128)} %select_bitcast_fusion) | data formatting | bytes 12960000 | tf_op jit(solution)/shard_map/transpose | solution.py:117
  509.2 18.1 %reshape.115 = f32[30,300,180]{2,1,0:T(8,128)} reshape(f32[30,6,50,3,60]{4,3,2,1,0:T(4,128)} %copy.396) | data formatting | bytes 12960000 | tf_op jit(solution)/shard_map/reshape | solution.py:118
  531.8 4.4 slice_maximum_fusion
  536.3 4.5 pad_maximum_fusion
  540.8 8.8 fusion.301
  572.3 5.8 fusion.5
  579.0 32.6 %fusion.8 = (f32[300,180]{1,0:T(8,128)S(1)}, f32[300,180]{1,0:T(8,128)S(1)}, f32[300,180]{1,0:T(8,128)}) fusion(f32[30,300,180]{2,1,0:T(8,128)S(1)} %bitcast.710, f32[31,302,1]{2,1,0:T(8,128)S(1)} %copy-done.1, f32[31,1,180]{2,1,0:T(1,128)S(1)} %collective-permute-done.1, f32[31,1,180]{2,1,0:T(1,128)S(1)} %collective-permute-done, ...), kind=kLoop, calls=%fused_computation.19 | loop fusion | flops 35478000 | bytes 8133856 | tf_op jit(solution)/shard_map/reduce_sum | solution.py:198
  629.1 39.4 %all-reduce = (f32[]{:T(128)}, f32[]{:T(128)}) all-reduce(f32[]{:T(128)} %get-tuple-element.24, f32[]{:T(128)} %get-tuple-element.23), channel_id=1, replica_groups=mesh['gx'=8,'gy'=4] {'gx','gy'}, use_global_device_ids=true, to_apply=%region_10.11 | all-reduce | flops 2 | bytes 16 | tf_op jit(solution)/shard_map/psum | solution.py:139
  670.6 40.4 %psum.44 = f32[]{:T(128)} all-reduce(f32[]{:T(128)} %get-tuple-element.34), channel_id=1, replica_groups=mesh['gx'=8,'gy'=4] {'gx','gy'}, use_global_device_ids=true, to_apply=%region_14.15 | all-reduce | flops 1 | bytes 8 | tf_op jit(solution)/shard_map/psum | solution.py:139
  725.0 4.5 collective-permute-done.20
  731.6 39.6 %psum.45 = f32[]{:T(128)} all-reduce(f32[]{:T(128)} %get-tuple-element.32), channel_id=1, replica_groups=mesh['gx'=8,'gy'=4] {'gx','gy'}, use_global_device_ids=true, to_apply=%region_16.17 | all-reduce | flops 1 | bytes 8 | tf_op jit(solution)/shard_map/psum | solution.py:219
  774.1 40.7 %psum.46 = f32[]{:T(128)} all-reduce(f32[]{:T(128)} %get-tuple-element.29), channel_id=1, replica_groups=mesh['gx'=8,'gy'=4] {'gx','gy'}, use_global_device_ids=true, to_apply=%region_18.19 | all-reduce | flops 1 | bytes 8 | tf_op jit(solution)/shard_map/psum | solution.py:139
  828.5 4.5 collective-permute-done.27
  835.2 39.4 %psum.47 = f32[]{:T(128)} all-reduce(f32[]{:T(128)} %get-tuple-element.27), channel_id=1, replica_groups=mesh['gx'=8,'gy'=4] {'gx','gy'}, use_global_device_ids=true, to_apply=%region_20.21 | all-reduce | flops 1 | bytes 8 | tf_op jit(solution)/shard_map/psum | solution.py:219
  (472 shorter events, 179.4 us)
Async XLA Ops:
  0.6 38.9 %slice-start.3 = ((s8[7077888]{0:T(1024)(128)(4,1)}), s8[2883584]{0:T(1024)(128)(4,1)S(1)}, s32[]{:S(2)}) async-start(s8[7077888]{0:T(1024)(128)(4,1)} %bitcast.723), calls=%async_computation.5 | async-start | bytes 5767168
  5.0 240.6 %all-to-all-start = ((s32[8,3,1]{1,2,0:T(1,128)}), s32[8,3,1]{1,2,0:T(1,128)S(1)}, u32[]{:S(2)}, u32[]{:S(2)}) async-start(s32[8,3,1]{1,2,0:T(1,128)} %bitcast.151), calls=%async_computation | async-start | bytes 8192 | tf_op jit(solution)/shard_map/all_to_all | solution.py:181
  60.5 39.9 %copy-start.12 = (f32[18,3000]{1,0:T(8,128)}, f32[18,3000]{1,0:T(8,128)S(1)}, u32[]{:S(2)}) copy-start(f32[18,3000]{1,0:T(8,128)S(1)} %get-tuple-element.206) | copy-start | bytes 648004
  245.6 211.2 %all-to-all-start.1 = ((f32[24,30,3000]{2,1,0:T(8,128)}), f32[24,30,3000]{2,1,0:T(8,128)}, u32[]{:S(2)}, u32[]{:S(2)}) async-start(f32[24,30,3000]{2,1,0:T(8,128)} %select_select_fusion), calls=%async_computation.1 | async-start | bytes 18874368 | tf_op jit(solution)/shard_map/all_to_all | solution.py:180
  528.6 7.7 collective-permute-start
  528.6 7.6 collective-permute-start.1
  530.4 5.9 collective-permute-start.4
  536.2 25.4 %collective-permute-start.5 = (f32[31,180]{1,0:T(8,128)S(1)}, f32[31,180]{1,0:T(8,128)S(1)}, u32[]{:S(2)}, u32[]{:S(2)}) collective-permute-start(f32[31,180]{1,0:T(8,128)S(1)} %collective-permute-done.4), channel_id=1, source_target_pairs={{0,8},{4,12},{8,0},{12,4},{16,24},{20,28},{24,16},{28,20},{1,9},{5... | collective-permute-start | bytes 66968 | tf_op jit(solution)/shard_map/ppermute | solution.py:22
  553.2 8.8 %collective-permute-start.3 = (f32[31,302,1]{1,2,0:T(1,128)S(1)}, f32[31,302,1]{1,2,0:T(1,128)S(1)}, u32[]{:S(2)}, u32[]{:S(2)}) collective-permute-start(f32[31,302,1]{1,2,0:T(1,128)S(1)} %copy.399), channel_id=1, source_target_pairs={{0,4},{4,8},{8,12},{12,16},{16,20},{20,24},{24,28},{28,0},{1,5},{5... | collective-permute-start | bytes 112352 | tf_op jit(solution)/shard_map/ppermute | solution.py:32
  557.6 7.6 collective-permute-start.2
  561.6 6.7 collective-permute-start.6
  613.0 5.4 collective-permute-start.7
  613.1 5.3 collective-permute-start.8
  614.8 3.6 collective-permute-start.11
  618.4 5.0 collective-permute-start.12
  618.5 9.5 %collective-permute-start.10 = (f32[1,302,1]{2,1,0:T(8,128)S(1)}, f32[1,302,1]{2,1,0:T(8,128)S(1)}, u32[]{:S(2)}, u32[]{:S(2)}) collective-permute-start(f32[1,302,1]{2,1,0:T(8,128)S(1)} %get-tuple-element.298), channel_id=1, source_target_pairs={{0,4},{4,8},{8,12},{12,16},{16,20},{20,24},{24,28},{28,0},{1,5},{5... | collective-permute-start | bytes 3632 | tf_op jit(solution)/shard_map/ppermute | solution.py:32
  619.9 8.3 collective-permute-start.9
  623.3 4.5 collective-permute-start.13
  712.4 7.0 collective-permute-start.14
  712.5 7.0 collective-permute-start.15
  714.2 3.8 collective-permute-start.18
  718.0 7.0 collective-permute-start.19
  720.3 9.5 %collective-permute-start.17 = (f32[1,302,1]{2,1,0:T(8,128)}, f32[1,302,1]{2,1,0:T(8,128)S(1)}, u32[]{:S(2)}, u32[]{:S(2)}) collective-permute-start(f32[1,302,1]{2,1,0:T(8,128)} %get-tuple-element.292), channel_id=1, source_target_pairs={{0,4},{4,8},{8,12},{12,16},{16,20},{20,24},{24,28},{28,0},{1,5},{5... | collective-permute-start | bytes 3632 | tf_op jit(solution)/shard_map/ppermute | solution.py:32
  722.3 7.6 collective-permute-start.16
  725.0 4.5 collective-permute-start.20
  816.2 6.7 collective-permute-start.21
  816.3 6.6 collective-permute-start.22
  818.0 3.8 collective-permute-start.25
  821.8 6.6 collective-permute-start.26
  823.7 9.5 %collective-permute-start.24 = (f32[1,302,1]{2,1,0:T(8,128)}, f32[1,302,1]{2,1,0:T(8,128)S(1)}, u32[]{:S(2)}, u32[]{:S(2)}) collective-permute-start(f32[1,302,1]{2,1,0:T(8,128)} %get-tuple-element.286), channel_id=1, source_target_pairs={{0,4},{4,8},{8,12},{12,16},{16,20},{20,24},{24,28},{28,0},{1,5},{5... | collective-permute-start | bytes 3632 | tf_op jit(solution)/shard_map/ppermute | solution.py:32
  825.7 7.8 collective-permute-start.23
  828.4 4.5 collective-permute-start.27
  (120 other events, 2314.5 us)
where the time goes:
time: 894 us; the launch traced here: 879 us
  local copies, waits for them, and re-layouts  262 us (29%)
  blocking collectives  200 us (22%)
  other arithmetic  179 us (20%)
  waiting for transfers between devices  179 us (20%)
  starting transfers between devices  50 us (6%)
  between operations  8.96 us (1%)
    all_to_all x1, waiting for transfers between devices, on_device(): lax.all_to_all(send_cols, 'gx', split_axis=0, concat_axis=0, tiled=True)  160 us
    psum x3, blocking collectives, global_sum(): return lax.psum(jnp.sum(values), ('gx', 'gy'))  121 us
    psum x2, blocking collectives, on_device(): lax.psum(jnp.sum(direction * result), ('gx', 'gy'))  79 us
    unnamed x310, local copies, waits for them, and re-layouts  76.2 us
    another operation x31, local copies, waits for them, and re-layouts, weight_balanced(): return jnp.stack(layers_out, axis=1)  60.8 us
    reduce_sum x2, other arithmetic, on_device(): jnp.sum(jnp.where(layer_index < face_levels, neighbour[:-1] - region, 0.0...  38.5 us
    add x1, other arithmetic, weight_balanced(): running = running + mass_per_volume  32.8 us
    div x2, other arithmetic, thomas_vertical_inverse(): salt_rows.append(salt_term / pivots)  26.2 us
  transfers between devices with their start and end apart: 30, of which 10 were waited for; matrix products, arithmetic and copies ran while one was open for 35% of the time, Pallas kernels for 0%

commit v1 on v0

v1 whole, which is shorter than its diff:
```python
import functools
import numpy as np
import jax
import jax.numpy as jnp
from jax import lax
from jax.experimental import pallas as pl
from jax.experimental.pallas import tpu as pltpu
from jax.sharding import PartitionSpec as P

SPAN_E = 60
SPAN_N = 50
KX = 3
KY = 6
LEVELS = 30
HALINE = 0.8
THERMAL = 0.6
RATIO = THERMAL / HALINE
DAMPING = 0.05
COLS = SPAN_E * SPAN_N
TILES = 24
SLOT_ROWS = 24
STEP = 25
PITCH = 33
EDGE = 384
FLAT = TILES * 128
RY = KY * SPAN_N
RX = KX * SPAN_E
GY = 312
GX = 256
F32 = jnp.float32
MIB = 2**20


def widths():
    return [(c, min(128, COLS - 128 * c)) for c in range(TILES)]


def vm():
    return pl.BlockSpec(memory_space=pltpu.VMEM)


def sm():
    return pl.BlockSpec(memory_space=pltpu.SMEM)


def hbm():
    return pl.BlockSpec(memory_space=pltpu.HBM)


def divide(x, d):
    return (x * (2**20 // d + 1)) >> 20


def coefficient(coef, kind, k):
    return coef[8 * (kind * LEVELS + k) : 8 * (kind * LEVELS + k) + 8, :]


def fill_coefficients(mixing, coef):
    ones = jnp.ones((8, 128), F32)
    base = ones
    for k in range(LEVELS):
        last = 8 * (2 * LEVELS + k)
        coef[last : last + 8, :] = ones / base
        if k + 1 < LEVELS:
            here = jnp.full((8, 128), mixing[k], F32)
            q = ones / (base + here)
            g = here * q
            coef[8 * k : 8 * k + 8, :] = g
            coef[8 * (LEVELS + k) : 8 * (LEVELS + k) + 8, :] = q
            base = ones + here - here * g


def spread_slots(rows, slots_by_column):
    for c, w in widths():
        rows[c * STEP : c * STEP + slots_by_column.shape[0], 0:w] = slots_by_column[:, c * 128 : c * 128 + w]


def pieces_of(rows, start, step):
    return [rows[pl.ds(u * 8 * step + start, 8, stride=step), :] for u in range(TILES // 8)]


MID = 25


ROW_SIZE = TILES * PITCH + 8
MID_SIZE = 32 * MID + 8


def copy_in(rows, base, values):
    for c, w in widths():
        rows[base + c * PITCH : base + c * PITCH + LEVELS, 0:w] = values(c, w)


def level_at(j, k, u):
    start = j * MID_SIZE + k * MID + u * 8
    return slice(start, start + 8)


def columns_at(j, k, u):
    return pl.ds(j * ROW_SIZE + u * 8 * PITCH + k, 8, stride=PITCH)


def solve_body(first, group, extra, warm, salt, n_rows, q_rows, coef, *rest):
    warm_out, salt_out, _, warm_rows, salt_rows, warm_mid, salt_mid = rest[extra:]
    step = pl.program_id(0)
    many = range(group)
    each = [(j, u) for j in many for u in range(TILES // 8)]
    n, t, s = {}, {}, {}
    for j in many:
        copy_in(warm_rows, j * ROW_SIZE, lambda c, w: warm[j, :, c * 128 : c * 128 + w])
        copy_in(salt_rows, j * ROW_SIZE, lambda c, w: salt[j, :, c * 128 : c * 128 + w])
        slot = first + step * group + j
        for u, deep in enumerate(pieces_of(n_rows, slot, STEP)):
            n[j, u] = deep
        for u, heat in enumerate(pieces_of(q_rows, slot, STEP)):
            t[j, u] = jnp.where(n[j, u] > 0, heat, 0.0)
    for k in range(LEVELS):
        g = coefficient(coef, 0, k - 1) if k else None
        for j, u in each:
            rt = warm_rows[columns_at(j, k, u), :]
            rs = salt_rows[columns_at(j, k, u), :]
            if k == 0:
                t[j, u] = rt + t[j, u]
                s[j, u] = rs
            else:
                e = jnp.where(n[j, u] > k, g, 0.0)
                t[j, u] = rt + e * t[j, u]
                s[j, u] = rs + e * s[j, u]
            warm_mid[level_at(j, k, u), :] = t[j, u]
            salt_mid[level_at(j, k, u), :] = s[j, u]
    for k in range(LEVELS - 1, -1, -1):
        last = coefficient(coef, 2, k)
        q = coefficient(coef, 1, k) if k + 1 < LEVELS else None
        g = coefficient(coef, 0, k) if k + 1 < LEVELS else None
        for j, u in each:
            a = jnp.where(n[j, u] > k, last, 1.0)
            if k + 1 < LEVELS:
                more = n[j, u] > k + 1
                a = jnp.where(more, q, a)
                e = jnp.where(more, g, 0.0)
                t[j, u] = a * warm_mid[level_at(j, k, u), :] + e * t[j, u]
                s[j, u] = a * salt_mid[level_at(j, k, u), :] + e * s[j, u]
            else:
                t[j, u] = a * t[j, u]
                s[j, u] = a * s[j, u]
            warm_mid[level_at(j, k, u), :] = t[j, u]
            salt_mid[level_at(j, k, u), :] = s[j, u]
    for j in many:
        for c, w in widths():
            for k in range(0, LEVELS, 8):
                h = min(8, LEVELS - k)
                part = pl.ds(j * MID_SIZE + k * MID + c, h, stride=MID)
                warm_out[j, k : k + h, c * 128 : c * 128 + w] = warm_mid[part, :][:, 0:w]
                salt_out[j, k : k + h, c * 128 : c * 128 + w] = salt_mid[part, :][:, 0:w]


def mark_shape():
    return jax.ShapeDtypeStruct((8, 128), F32)


def coefficient_shape():
    return (3 * LEVELS * 8, 128)


def solve_columns(warm, salt, columns, first, count, before, after):
    group = 3 if first % 3 == 0 and count % 3 == 0 else 1
    block = pl.BlockSpec((group, LEVELS, COLS), lambda i: (first // group + i, 0, 0))
    extra = len(before) + len(after)
    return pl.pallas_call(
        functools.partial(solve_body, first, group, extra),
        grid=(count // group,),
        out_shape=(jax.ShapeDtypeStruct(warm.shape, F32), jax.ShapeDtypeStruct(salt.shape, F32), mark_shape()),
        in_specs=[block, block] + [vm()] * 3 + [hbm()] * extra,
        out_specs=(block, block, hbm()),
        scratch_shapes=[
            pltpu.VMEM((group * ROW_SIZE, 128), F32),
            pltpu.VMEM((group * ROW_SIZE, 128), F32),
            pltpu.VMEM((group * MID_SIZE, 128), F32),
            pltpu.VMEM((group * MID_SIZE, 128), F32),
        ],
        input_output_aliases={5: 0, 6: 1} if before else {},
        compiler_params=pltpu.CompilerParams(vmem_limit_bytes=49 * MIB),
        cost_estimate=pl.CostEstimate(flops=count * 2_000_000, bytes_accessed=count * 1_600_000, transcendentals=0),
        name="column_solve",
    )(warm, salt, *columns, *before, *after)


def rim_sources():
    lane = lax.broadcasted_iota(jnp.int32, (8, 128), 1)
    one = jnp.where(lane < 64, lane, lane - 64)
    along_x = jnp.where(one < SPAN_N, one * SPAN_E + jnp.where(lane < 64, 0, SPAN_E - 1), -1)
    along_y = jnp.where(one < SPAN_E, one + jnp.where(lane < 64, 0, COLS - SPAN_E), -1)
    return along_x, along_y


def lanes_of(x, index):
    return jnp.take_along_axis(x, index, axis=1, mode="promise_in_bounds")


def rim_of(tile):
    sources = rim_sources()
    used = (range(TILES), (0, TILES - 2, TILES - 1))
    out = [None, None]
    for c in range(TILES):
        now = tile(c)
        for d in range(2):
            if c in used[d]:
                before = out[d] or [jnp.zeros((8, 128), F32)] * len(now)
                here = (sources[d] >> 7) == c
                out[d] = [jnp.where(here, lanes_of(v, sources[d] & 127), p) for v, p in zip(now, before)]
    return out


def tables_body(span_x, span_y, mixing, ids, depth, inflow, after, *rest):
    n_rows, q_rows, coef, pick, rim_x, rim_y, listed, padded = rest
    slots = depth.shape[0]
    n_rows[...] = jnp.zeros(n_rows.shape, jnp.int32)
    spread_slots(n_rows, depth)
    spread_slots(q_rows, inflow)
    fill_coefficients(mixing, coef)
    padded[...] = jnp.zeros((SLOT_ROWS, FLAT), F32)
    padded[0:slots, 0:COLS] = depth[...].astype(F32)
    rims = rim_of(lambda c: [padded[8 * g : 8 * g + 8, c * 128 : c * 128 + 128] for g in range(SLOT_ROWS // 8)])
    for ref, parts in zip((rim_x, rim_y), rims):
        ref[...] = jnp.concatenate(parts, axis=0)
    blocks_x = KX * span_x
    row = lax.broadcasted_iota(jnp.int32, (SLOT_ROWS, 128), 0)
    held = jnp.zeros((SLOT_ROWS, 128), jnp.int32)
    for s in range(slots):
        held = jnp.where(row == s, jnp.maximum(ids[s], 0), held)
    lane = lax.broadcasted_iota(jnp.int32, (8, 128), 1)
    line = jnp.full((8, 128), -1.0, F32)
    for s in range(slots):
        line = jnp.where(lane == s, ids[s].astype(F32), line)
    listed[...] = line
    up = divide(held, blocks_x)
    across = held - blocks_x * up
    band = up - KY * divide(up, KY)

    def spot(b, m, folds=False):
        o = divide(b, KX)
        c = b - KX * o
        return jnp.where(folds, span_x - 1 - o, o) * 32 + c * 8 + m

    spots = (
        spot(jnp.where(across == 0, blocks_x, across) - 1, band + 1),
        spot(jnp.where(across == blocks_x - 1, -1, across) + 1, band + 1),
        spot(across, band),
        spot(across, band + 2, up == KY * span_y - 1),
    )
    at = lax.broadcasted_iota(jnp.int32, (SLOT_ROWS, 128), 1)
    for d, where in enumerate(spots):
        for t in range(span_x * 32 // 128):
            pick[d * SLOT_ROWS : (d + 1) * SLOT_ROWS, t * 128 : t * 128 + 128] = jnp.where(
                at + t * 128 == where, 1.0, 0.0
            )


def column_tables(span_x, span_y, mixing, ids, depth, inflow, after):
    rows = (TILES * STEP + 8, 128)
    return pl.pallas_call(
        functools.partial(tables_body, span_x, span_y),
        out_shape=(
            jax.ShapeDtypeStruct(rows, jnp.int32),
            jax.ShapeDtypeStruct(rows, F32),
            jax.ShapeDtypeStruct(coefficient_shape(), F32),
        )
        + (jax.ShapeDtypeStruct((4 * SLOT_ROWS, span_x * 32), F32),)
        + (jax.ShapeDtypeStruct((SLOT_ROWS, 128), F32),) * 2
        + (jax.ShapeDtypeStruct((8, 128), F32),),
        in_specs=[sm(), sm(), vm(), vm(), hbm()],
        out_specs=(vm(),) * 7,
        scratch_shapes=[pltpu.VMEM((SLOT_ROWS, FLAT), F32)],
        compiler_params=pltpu.CompilerParams(vmem_limit_bytes=12 * MIB),
        cost_estimate=pl.CostEstimate(flops=5_000_000, bytes_accessed=3_000_000, transcendentals=0),
        name="column_tables",
    )(mixing, ids, depth, inflow, after)


def spread_lines(span_y, top, bottom, out):
    here = lax.axis_index("gy")
    for p in range(span_y):
        out[p] = jnp.where(here == p - 1, top, jnp.where(here == p + 1, bottom, 0.0))


def beside_lines(span_y, lines, folded):
    here = lax.axis_index("gy")
    ups = jnp.where(here == span_y - 1, folded, lines[jnp.minimum(here + 1, span_y - 1)])
    downs = jnp.where(here == 0, 0.0, lines[jnp.maximum(here - 1, 0)])
    return ups, downs


def edges_body(span_x, span_y, depth, lines, held, table, extended, _, rows):
    ups, downs = beside_lines(span_y, lines, 0.0)
    top = lax.axis_index("gy") == span_y - 1
    extended[...] = depth[...]
    extended[RY : RY + 4, :] = ups[0:4]
    extended[GY - 4 : GY, :] = downs[0:4]
    lane = lax.broadcasted_iota(jnp.int32, (8, GX), 1)
    pick = lax.broadcasted_iota(jnp.int32, (8, GX), 0)
    ext16 = extended[...].astype(jnp.bfloat16)

    def columns(wanted):
        hot = jnp.where(lane == wanted, 1.0, 0.0).astype(jnp.bfloat16)
        out = lax.dot_general(hot, ext16, (((1,), (1,)), ((), ())), preferred_element_type=F32)
        return jnp.concatenate([out, jnp.zeros((8, EDGE - GY), F32)], axis=1)

    sides = columns(jnp.where(pick < 3, pick * SPAN_E, jnp.where(pick < 6, (pick - 3) * SPAN_E + SPAN_E - 1, -1)))
    rows[...] = jnp.zeros((16, GX), F32)
    for m in range(KY + 1):
        rows[m + 1 : m + 2, :] = extended[m * SPAN_N : m * SPAN_N + 1, :]
        y = m * SPAN_N - 1 if m else GY - 1
        rows[8 + m : 9 + m, :] = extended[y : y + 1, :]
    turned = turn(jnp.concatenate([extended[RY - 1 - y : RY - y, :] for y in range(4)] * 2, axis=0))
    rows[KY + 1 : KY + 2, :] = jnp.where(top, turned[0:1], rows[KY + 1 : KY + 2, :])
    low = rows[0:8, :]
    high = rows[8:16, :]
    lane1 = lane[:, 0:128]
    for b in range(KX):
        a = pltpu.roll(low, (192 - b * SPAN_E) % GX, 1)
        z = pltpu.roll(high, (128 - b * SPAN_E) % GX, 1)
        both = jnp.where(lane >= 192, a, z)
        table[0, 8 * b : 8 * b + 8, 128:256] = both[:, 128:256]
        table[0, 8 * b : 8 * b + 8, 0:128] = jnp.zeros((8, 128), F32)
        table[0, 8 * b : 8 * b + 8, 256:384] = jnp.zeros((8, 128), F32)
    for m in range(KY):
        z = pltpu.roll(sides, (EDGE - m * SPAN_N) % EDGE, 1)[:, 0:128]
        a = pltpu.roll(sides, (EDGE + 64 - m * SPAN_N) % EDGE, 1)[:, 0:128]
        for b in range(KX):
            table[0, 8 * b + m + 1 : 8 * b + m + 2, 0:128] = jnp.where(
                lane1[0:1] >= 64, a[b : b + 1], z[3 + b : 4 + b]
            )
    table[0, 0:1, 256:384] = held[0:1, :]
    table[0, 8:12, 256:384] = turned[0:4, 0:128]
    table[0, 12:16, 256:384] = turned[0:4, 128:256]
    table[0, 24:32, :] = columns(jnp.where(pick < 4, pick, RX - 8 + pick))
    for d in range(1, span_x):
        table[d] = table[0]


def block_edges(span_x, span_y, depth, lines, held):
    return pl.pallas_call(
        functools.partial(edges_body, span_x, span_y),
        out_shape=(
            jax.ShapeDtypeStruct((span_x, 32, EDGE), F32),
            jax.ShapeDtypeStruct((GY, GX), F32),
            mark_shape(),
        ),
        in_specs=[vm()] * 3,
        out_specs=(vm(),) * 2 + (hbm(),),
        scratch_shapes=[pltpu.VMEM((16, GX), F32)],
        compiler_params=pltpu.CompilerParams(vmem_limit_bytes=12 * MIB),
        name="block_edges",
    )(depth, lines, held)


def ends_body(span_y, depth, region, out, wide):
    wide[...] = jnp.zeros(wide.shape, F32)
    wide[0:RX, 0:RY] = depth[...].astype(F32)
    region[...] = wide[...].T[0:GY, :]

    def lines(first):
        return jnp.concatenate([region[first : first + 4, :], jnp.zeros((4, GX), F32)], axis=0)

    spread_lines(span_y, lines(RY - 4), lines(0), out)


def region_ends(span_y, depth_t):
    return pl.pallas_call(
        functools.partial(ends_body, span_y),
        out_shape=(
            jax.ShapeDtypeStruct((GY, GX), F32),
            jax.ShapeDtypeStruct((span_y, 8, GX), F32),
        ),
        in_specs=[vm()],
        out_specs=(vm(),) * 2,
        scratch_shapes=[pltpu.VMEM((GX, EDGE), F32)],
        compiler_params=pltpu.CompilerParams(vmem_limit_bytes=12 * MIB),
        name="region_ends",
    )(depth_t)


ROWS = 40
HALF = 13


SLOT_STEP = 201


def shifted(x, by):
    rows = x.shape[0]
    lane = lax.broadcasted_iota(jnp.int32, x.shape, 1)
    near = pltpu.roll(x, -by % 128, 1)
    far = pltpu.roll(near, (rows - 1) if by > 0 else 1, 0)
    return jnp.where(lane < 128 - by if by > 0 else lane >= -by, near, far)


def flux_body(
    slots, group, warm, salt, n_rows, q_rows, coef, after, pieces, rim_x, rim_y,
    faces, found, rows, middle, totals,
):
    step = pl.program_id(0)
    lane = lax.broadcasted_iota(jnp.int32, (1, FLAT), 1)
    col = lane - SPAN_E * divide(lane, SPAN_E)

    @pl.when(step == 0)
    def _():
        faces[...] = jnp.zeros(faces.shape, jnp.int32)

    many = range(group)
    each = [(j, u) for j in many for u in range(TILES // 8)]
    place = lax.broadcasted_iota(jnp.int32, (TILES, 128), 0) * 128
    place = place + lax.broadcasted_iota(jnp.int32, (TILES, 128), 1)
    in_row = place - SPAN_E * divide(place, SPAN_E)
    n, x = {}, {}
    for j in many:
        copy_in(
            rows,
            j * ROW_SIZE,
            lambda c, w: salt[j, :, c * 128 : c * 128 + w] - RATIO * warm[j, :, c * 128 : c * 128 + w],
        )
        slot = step * group + j
        for u, deep in enumerate(pieces_of(n_rows, slot, STEP)):
            n[j, u] = deep
        for u, heat in enumerate(pieces_of(q_rows, slot, STEP)):
            x[j, u] = RATIO * heat
        deep = jnp.concatenate([n[j, u] for u in range(TILES // 8)], axis=0)
        for d, (by, inside) in enumerate(
            (
                (1, in_row < SPAN_E - 1),
                (-1, in_row > 0),
                (SPAN_E, place < COLS - SPAN_E),
                (-SPAN_E, place >= SPAN_E),
            )
        ):
            start = (8 * j + d) * MID
            faces[start : start + TILES, :] = jnp.where(inside, jnp.minimum(deep, shifted(deep, by)), 0)
    for k in range(LEVELS):
        g = coefficient(coef, 0, k - 1) if k else None
        for j, u in each:
            right = rows[columns_at(j, k, u), :]
            x[j, u] = right + g * x[j, u] if k else right - x[j, u]
            middle[j, k, u * 8 : u * 8 + 8, :] = x[j, u]
    for k in range(LEVELS - 1, -1, -1):
        last = coefficient(coef, 2, k)
        q = coefficient(coef, 1, k) if k + 1 < LEVELS else None
        g = coefficient(coef, 0, k) if k + 1 < LEVELS else None
        for j, u in each:
            if k + 1 < LEVELS:
                more = n[j, u] > k + 1
                a = jnp.where(more, q, last)
                e = jnp.where(more, g, 0.0)
                x[j, u] = a * middle[j, k, u * 8 : u * 8 + 8, :] + e * x[j, u]
            else:
                x[j, u] = last * x[j, u]
            middle[j, k, u * 8 : u * 8 + 8, :] = x[j, u]
    zero = jnp.zeros((8, 128), F32)
    pressure = {at: zero for at in each}
    total = {at: zero for at in each}
    for k in range(LEVELS):
        for j, u in each:
            pressure[j, u] = pressure[j, u] + middle[j, k, u * 8 : u * 8 + 8, :]
            total[j, u] = total[j, u] + pressure[j, u]
            totals[level_at(j, k, u), :] = total[j, u]

    for j in many:
        slot = step * group + j

        def tile(c):
            now = [totals[pl.ds(j * MID_SIZE + 8 * g * MID + c, 8, stride=MID), :] for g in range(4)]
            level = faces[pl.ds(8 * j * MID + c, 8, stride=MID), :] - 1
            sums = zero
            for g in range(4):
                one_of = jnp.take_along_axis(now[g], level & 7, axis=0, mode="promise_in_bounds")
                sums = jnp.where((level >> 3) == g, one_of, sums)
            found[pl.ds(slot * SLOT_STEP + c * 8, 8), :] = sums
            return now

        for ref, parts in zip((rim_x, rim_y), rim_of(tile)):
            for g in range(4):
                ref[j, 8 * g : 8 * g + 8, :] = parts[g]

    @pl.when(step == slots // group - 1)
    def _():
        def flat(d):
            return jnp.concatenate(
                [found[pl.ds(c * 8 + d, SLOT_ROWS, stride=SLOT_STEP), :] for c in range(TILES)], axis=1
            )

        east, west, north, south = (flat(d) for d in range(4))
        from_east = pltpu.roll(west, FLAT - 1, 1)
        from_west = pltpu.roll(east, 1, 1)
        net = -(east + west + north + south)
        net = net + jnp.where(col < SPAN_E - 1, from_east, 0.0)
        net = net + jnp.where(col > 0, from_west, 0.0)
        net = net + jnp.where(lane < COLS - SPAN_E, pltpu.roll(south, FLAT - SPAN_E, 1), 0.0)
        net = net + jnp.where(lane >= SPAN_E, pltpu.roll(north, SPAN_E, 1), 0.0)
        l = lax.broadcasted_iota(jnp.int32, (1, 128), 1)
        for t in range(26):
            halves = []
            for h in range(2):
                r = 2 * t + h
                if r in (0, SPAN_N + 1):
                    continue
                start = (r - 1) * SPAN_E
                a = start // 128
                row = net[:, a * 128 : a * 128 + 128]
                if start % 128 + SPAN_E > 128:
                    row = jnp.where(l >= start % 128, row, net[:, a * 128 + 128 : a * 128 + 256])
                row = pltpu.roll(row, (64 * h + 1 - start) % 128, 1)
                halves.append(jnp.where((l > 64 * h) & (l <= 64 * h + SPAN_E), row, 0.0))
            pieces[t * STEP : t * STEP + SLOT_ROWS, :] = halves[0] + halves[1] if len(halves) == 2 else halves[0]


def face_sums(warm, salt, columns, after):
    slots = warm.shape[0]
    group = 3 if slots % 3 == 0 else 1
    block = pl.BlockSpec((group, LEVELS, COLS), lambda i: (i, 0, 0))
    rim = pl.BlockSpec((group, 32, 128), lambda i: (i, 0, 0))
    return pl.pallas_call(
        functools.partial(flux_body, slots, group),
        grid=(slots // group,),
        out_shape=(jax.ShapeDtypeStruct((26 * STEP + 6, 128), F32),)
        + (jax.ShapeDtypeStruct((slots, 32, 128), F32),) * 2,
        in_specs=[block, block] + [vm()] * 3 + [hbm()],
        out_specs=(vm(), rim, rim),
        scratch_shapes=[
            pltpu.VMEM((8 * group * MID, 128), jnp.int32),
            pltpu.VMEM((SLOT_ROWS * SLOT_STEP, 128), F32),
            pltpu.VMEM((group * ROW_SIZE, 128), F32),
            pltpu.VMEM((group, LEVELS, TILES, 128), F32),
            pltpu.VMEM((group * MID_SIZE, 128), F32),
        ],
        compiler_params=pltpu.CompilerParams(vmem_limit_bytes=49 * MIB),
        cost_estimate=pl.CostEstimate(flops=40_000_000, bytes_accessed=15_000_000, transcendentals=0),
        name="face_sums",
    )(warm, salt, *columns, after)


def received_rows(span_x, cap, edges):
    blocks_x = KX * span_x
    keys = jnp.concatenate([edges[d * 32 : d * 32 + 1, 256:384] for d in range(span_x)], axis=0).astype(jnp.int32)
    held = jnp.maximum(keys, 0)
    owner = jnp.where(keys >= 0, divide(held - blocks_x * divide(held, blocks_x), KX), -1)
    one_of = [jnp.where(owner == o, 1.0, 0.0) for o in range(span_x)]
    earlier = lax.broadcasted_iota(jnp.int32, (128, 128), 0) < lax.broadcasted_iota(jnp.int32, (128, 128), 1)
    counted = jnp.dot(
        jnp.concatenate(one_of, axis=0).astype(jnp.bfloat16),
        jnp.where(earlier, 1.0, 0.0).astype(jnp.bfloat16),
        preferred_element_type=F32,
    )
    at = lax.broadcasted_iota(jnp.int32, (span_x, 128), 0).astype(F32) * cap + 1.0
    for o in range(span_x):
        at = at + one_of[o] * counted[o * span_x : (o + 1) * span_x]
    here_x = lax.axis_index("gx")
    first = lax.axis_index("gy") * KY

    def beside(x):
        x = jnp.where(x < 0, x + blocks_x, x)
        return jnp.where(x >= blocks_x, x - blocks_x, x)

    base = here_x * KX
    over = (span_x - 1 - here_x) * KX
    wanted = [(first + p // KX) * blocks_x + base + p % KX for p in range(KX * KY)]
    wanted += [(first + p) * blocks_x + beside(base - 1) for p in range(KY)]
    wanted += [(first + p) * blocks_x + beside(base + KX) for p in range(KY)]
    wanted += [(first + KY - 1) * blocks_x + x for x in [over + g for g in range(KX)]]
    wanted += [(first + KY - 1) * blocks_x + beside(x) for x in (over - 1, over + KX)]
    lines = [jnp.sum(jnp.where(keys == w, at, 0.0), axis=0, keepdims=True) for w in wanted]
    lines += [jnp.zeros((1, 128), F32)] * (ROWS - len(lines))
    sums = jnp.sum(jnp.concatenate(lines, axis=0), axis=1, keepdims=True) - 1.0
    return jnp.broadcast_to(sums, (ROWS, 128)).astype(jnp.int32)


def outgoing_body(
    span_x, cap, slots, ids, pick, edges, n_x, n_y, inside, rim_x, rim_y, out, rows, _, pieces, q_x, q_y, source, counts
):
    blocks_x = KX * span_x
    for d in range(span_x):
        counts[d] = 0
    for d in range(span_x * cap):
        source[d] = 0
    for s in range(slots):
        held = jnp.maximum(ids[s], 0)
        owner = divide(held - blocks_x * divide(held, blocks_x), KX)
        rank = counts[owner]

        @pl.when(ids[s] >= 0)
        def _():
            source[owner * cap + jnp.minimum(rank, cap - 1)] = s
            counts[owner] = rank + 1

    rows[...] = received_rows(span_x, cap, edges)
    near = jnp.dot(
        pick[...].astype(jnp.bfloat16), edges[:, 0:GX].astype(jnp.bfloat16), preferred_element_type=F32
    )
    l = lax.broadcasted_iota(jnp.int32, (1, 128), 1)
    w, e, so, no = (near[d * SLOT_ROWS : (d + 1) * SLOT_ROWS] for d in range(4))
    q_x[...] = jnp.zeros(q_x.shape, F32)
    q_y[...] = jnp.zeros(q_y.shape, F32)
    level = lax.broadcasted_iota(jnp.int32, (32, 128), 0).astype(F32) + 1.0
    for n, other, rim, q in (
        (n_x, jnp.where(l < 64, w[:, 0:128], e[:, 0:128]), rim_x, q_x),
        (n_y, jnp.where(l < 64, so[:, 128:256], no[:, 128:256]), rim_y, q_y),
    ):
        face = jnp.minimum(n[...], other)
        for s in range(slots):
            hit = jnp.where(face[s : s + 1] == level, rim[s], 0.0)
            q[s : s + 1, :] = jnp.sum(hit, axis=0, keepdims=True)

    groups = range(SLOT_ROWS // 8)
    lane = lax.broadcasted_iota(jnp.int32, (8, 128), 1)
    in_row = lane & 63
    odd = lane >> 6
    adds = jnp.where((in_row == 0) | (in_row == SPAN_E + 1), 1.0, 0.0)
    adds = jnp.where((in_row == 1) | (in_row == SPAN_E), -1.0, adds)
    zero = jnp.zeros((8, 128), F32)
    strips = [[[zero for _ in groups] for _ in range(2)] for _ in range(2)]
    for t in range(26):
        p, at = t // HALF, 4 * (t % HALF)
        i = 2 * t - 1 + odd
        index = jnp.clip(i, 0, SPAN_N - 1) + jnp.where(in_row >= 32, 64, 0)
        sign = jnp.where((i >= 0) & (i < SPAN_N), adds, 0.0)
        band = (in_row >= at) & (in_row < at + 4)
        for g in groups:
            rows8 = slice(8 * g, 8 * g + 8)
            v = inside[t * STEP + 8 * g : t * STEP + 8 * g + 8, :] + sign * lanes_of(q_x[rows8, :], index)
            core = (in_row >= 1) & (in_row <= SPAN_E)
            if t == 0:
                v = v + jnp.where(core & (odd == 0), pltpu.roll(q_y[rows8, :], 1, 1), 0.0)
                v = v - jnp.where(core & (odd == 1), pltpu.roll(q_y[rows8, :], 65, 1), 0.0)
            if t == 25:
                v = v - jnp.where(core & (odd == 0), pltpu.roll(q_y[rows8, :], 65, 1), 0.0)
                v = v + jnp.where(core & (odd == 1), pltpu.roll(q_y[rows8, :], 1, 1), 0.0)
            pieces[t * STEP + 8 * g : t * STEP + 8 * g + 8, :] = v
            strips[0][p][g] = jnp.where(band, pltpu.roll(v, at, 1), strips[0][p][g])
            strips[1][p][g] = jnp.where(band, pltpu.roll(v, (at - SPAN_E + 2) % 128, 1), strips[1][p][g])
    for side in range(2):
        for p in range(2):
            for g in groups:
                start = (26 + 2 * side + p) * STEP + 8 * g
                pieces[start : start + 8, :] = strips[side][p][g]
    pieces[30 * STEP : 32 * STEP + 8, :] = jnp.zeros((2 * STEP + 8, 128), F32)

    tile_row = lax.broadcasted_iota(jnp.int32, (8, 128), 0)
    corner = (in_row >= 52) & (in_row < 60)
    for d in range(span_x):
        for c in range(cap):
            other = span_x - 1 - d
            own = source[d * cap + c]
            left = source[(d - 1) % span_x * cap + c]
            right = source[(d + 1) % span_x * cap + c]
            fold = source[other * cap + c]
            fold_west = source[(other - 1) % span_x * cap + c]
            fold_east = source[(other + 1) % span_x * cap + c]

            def last(slot):
                return pieces[pl.ds(24 * STEP + slot, 8, stride=STEP), :]

            tail = jnp.where(tile_row < 2, last(own), jnp.where(tile_row < 4, last(right), last(left)))
            tail = jnp.where(tile_row >= 6, pltpu.roll(last(fold), 6, 0), tail)
            tail = jnp.where((tile_row == 3) & corner, pltpu.roll(last(fold_east), 8, 1), tail)
            tail = jnp.where((tile_row == 5) & corner, pltpu.roll(last(fold_west), 8, 1), tail)
            out[d * cap + c, 0:24, :] = pieces[pl.ds(own, 24, stride=STEP), :]
            out[d * cap + c, 24:32, :] = tail


def outgoing_blocks(span_x, cap, ids, pick, edges, rims, sums):
    slots = ids.shape[0]
    return pl.pallas_call(
        functools.partial(outgoing_body, span_x, cap, slots),
        out_shape=(
            jax.ShapeDtypeStruct((span_x * cap, 32, 128), F32),
            jax.ShapeDtypeStruct((ROWS, 128), jnp.int32),
            mark_shape(),
        ),
        in_specs=[sm()] + [vm()] * 7,
        out_specs=(vm(), vm(), hbm()),
        scratch_shapes=[pltpu.VMEM((32 * STEP + 8, 128), F32)]
        + [pltpu.VMEM((SLOT_ROWS, 128), F32)] * 2
        + [pltpu.SMEM((span_x * cap,), jnp.int32), pltpu.SMEM((span_x,), jnp.int32)],
        compiler_params=pltpu.CompilerParams(vmem_limit_bytes=12 * MIB),
        name="outgoing_blocks",
    )(ids, pick, edges, *rims, *sums)


def turn(x):
    lane = lax.broadcasted_iota(jnp.int32, (8, 128), 1)
    halves = [
        jnp.take_along_axis(x[:, h * 128 : h * 128 + 128], 127 - lane, axis=1, mode="promise_in_bounds")
        for h in (1, 0)
    ]
    return pltpu.roll(jnp.concatenate(halves, axis=1), (RX - GX) % GX, 1)


def region_body(span_y, rows, got, after, region, out, folded, tiles, sides):
    tiles[...] = jnp.zeros(tiles.shape, F32)
    sides[...] = jnp.zeros(sides.shape, F32)
    for p in range(KX * KY):
        r = rows[p, 0]
        block = got[pl.ds(pl.multiple_of(jnp.maximum(r, 0) * 32, 32), 32), :]
        block = jnp.where(r >= 0, block, 0.0)
        tiles[pl.ds((p % KX) * 8 + p // KX, 32, stride=STEP), :] = block
    for p in range(2 * KY):
        r = rows[KX * KY + p, 0]
        block = got[pl.ds(pl.multiple_of(jnp.maximum(r, 0) * 32 + 24, 8), 8), :]
        block = jnp.where(r >= 0, block, 0.0)
        sides[pl.ds((p // KY) * 8 + p % KY, 8, stride=17), :] = block
    at_fold = KX * KY + 2 * KY
    for g in range(KX + 2):
        r = rows[at_fold + g, 0]
        block = got[pl.ds(pl.multiple_of(jnp.maximum(r, 0) * 32 + 24, 8), 8), :]
        block = jnp.where(r >= 0, block, 0.0)
        if g < KX:
            for t in range(2):
                tiles[(24 + t) * STEP + g * 8 + 6 : (24 + t) * STEP + g * 8 + 7, :] = block[6 + t : 7 + t]
        elif g == KX:
            sides[5 * 17 + 6 : 5 * 17 + 7, :] = pltpu.roll(block, 120, 1)[5:6]
        else:
            sides[3 * 17 + 14 : 3 * 17 + 15, :] = pltpu.roll(block, 120, 1)[3:4]
    lane = lax.broadcasted_iota(jnp.int32, (8, 128), 1)
    sub = lax.broadcasted_iota(jnp.int32, (8, 128), 0)

    def assembled(r):
        t, base = r // 2, (r % 2) * 64
        v = [tiles[t * STEP + 8 * g : t * STEP + 8 * g + 8, :] for g in range(KX)]
        a = pltpu.roll(v[0], (-1 - base) % 128, 1)
        b = pltpu.roll(v[1], (59 - base) % 128, 1)
        c = pltpu.roll(v[2], (119 - base) % 128, 1)
        to = base + 4 * (t % HALF)
        p = t // HALF
        w = sides[(4 + p) * 17 : (4 + p) * 17 + 8, :]
        e = sides[(2 + p) * 17 + 8 : (2 + p) * 17 + 16, :]
        w = pltpu.roll(w, (125 - to) % 128, 1)
        e = pltpu.roll(e, (51 - to) % 128, 1)
        left = jnp.where(lane <= 60, a, 0.0)
        left = left + jnp.where((lane >= 59) & (lane <= 120), b, 0.0)
        left = left + jnp.where(lane >= 119, c, 0.0)
        left = left + jnp.where(lane == 0, w, 0.0)
        right = jnp.where(lane <= 52, c, 0.0)
        right = right + jnp.where(lane == 127, a, 0.0)
        right = right + jnp.where(lane >= 125, w, 0.0)
        right = right + jnp.where((lane >= 51) & (lane <= 54), e, 0.0)
        return left, right

    region[...] = jnp.zeros(region.shape, F32)
    below = assembled(0)
    above = assembled(SPAN_N + 1)
    over = [above]
    for r in range(1, SPAN_N + 1):
        parts = assembled(r)
        if r > SPAN_N - 3:
            over.insert(1, parts)
        for h in range(2):
            v = parts[h]
            if r == 1:
                v = v + jnp.where((sub >= 1) & (sub < KY), pltpu.roll(above[h], 1, 0), 0.0)
            if r == SPAN_N:
                v = v + jnp.where(sub < KY - 1, pltpu.roll(below[h], 7, 0), 0.0)
            region[pl.ds(h * GY + r - 1, KY, stride=SPAN_N), :] = v[0:KY]
    for h in range(2):
        region[h * GY + RY : h * GY + RY + 1, :] = above[h][KY - 1 : KY]
        region[h * GY + GY - 1 : h * GY + GY, :] = below[h][0:1]

    def lines(ys):
        cut = [
            jnp.concatenate([region[y : y + 1, :], region[GY + y : GY + y + 1, :]], axis=1) for y in ys
        ]
        return jnp.concatenate(cut + [jnp.zeros((8 - len(ys), GX), F32)], axis=0)

    spread_lines(span_y, lines([RY - 3, RY - 2, RY - 1, RY]), lines([GY - 1, 0, 1, 2]), out)
    over = [jnp.concatenate([part[6:7] for part in parts], axis=1) for parts in over]
    folded[...] = turn(jnp.concatenate(over + [jnp.zeros((4, GX), F32)], axis=0))


def region_sums(span_y, rows, got, after):
    return pl.pallas_call(
        functools.partial(region_body, span_y),
        out_shape=(
            jax.ShapeDtypeStruct((2 * GY, 128), F32),
            jax.ShapeDtypeStruct((span_y, 8, GX), F32),
            jax.ShapeDtypeStruct((8, GX), F32),
        ),
        in_specs=[sm(), vm(), hbm()],
        out_specs=(vm(),) * 3,
        scratch_shapes=[pltpu.VMEM((32 * STEP + 8, 128), F32), pltpu.VMEM((8 * 17, 128), F32)],
        compiler_params=pltpu.CompilerParams(vmem_limit_bytes=12 * MIB),
        name="region_sums",
    )(rows, got.reshape(-1, 128), after)


def basis_body(span_x, span_y, region, lines, folded, extended, edges, basis, diag_out, dots, mark):
    ext = extended[...]
    here = lax.axis_index("gx")
    lane8 = lax.broadcasted_iota(jnp.int32, (8, GX), 1)
    row8 = lax.broadcasted_iota(jnp.int32, (8, GX), 0)
    put_west = jnp.where((row8 >= 4) & (lane8 == GX - 8 + row8), 1.0, 0.0).astype(jnp.bfloat16)
    put_east = jnp.where((row8 < 4) & (lane8 == RX + row8), 1.0, 0.0).astype(jnp.bfloat16)
    for other, put in ((here + span_x - 1, put_west), (here + 1, put_east)):
        cols = edges[pl.ds(pl.multiple_of(other % span_x * 32 + 24, 8), 8), :]
        ext = ext + lax.dot_general(
            cols[:, 0:GY].astype(jnp.bfloat16), put, (((0,), (0,)), ((), ())), preferred_element_type=F32
        )

    fold = []
    for step in (0, -1, 1):
        other = span_x - 1 - here + step + span_x
        part = edges[pl.ds(pl.multiple_of(lax.rem(other, span_x) * 32 + 8, 8), 8), 256:384]
        fold.append(jnp.concatenate([part[0:4], part[4:8]], axis=1))
    lane4 = lax.broadcasted_iota(jnp.int32, (4, GX), 1)
    beyond = jnp.where(lane4 < RX, fold[0], 0.0)
    beyond = jnp.where((lane4 >= RX) & (lane4 < RX + 4), pltpu.roll(fold[1], RX, 1), beyond)
    beyond = jnp.where(lane4 >= GX - 4, pltpu.roll(fold[2], GX - RX, 1), beyond)
    beyond = jnp.where(lax.axis_index("gy") == span_y - 1, beyond, 0.0)
    ext = ext + jnp.concatenate([jnp.zeros((RY, GX), F32), beyond, jnp.zeros((GY - RY - 4, GX), F32)], axis=0)

    def south_of(x):
        return pltpu.roll(x, 1, 0)

    def north_of(x):
        return pltpu.roll(x, GY - 1, 0)

    def west_of(x):
        return pltpu.roll(x, 1, 1)

    def east_of(x):
        return pltpu.roll(x, GX - 1, 1)

    to_east = jnp.minimum(ext, east_of(ext)) / LEVELS
    to_north = jnp.minimum(ext, north_of(ext)) / LEVELS
    to_west = west_of(to_east)
    to_south = south_of(to_north)
    diagonal = jnp.where(ext > 0, DAMPING, 1.0) + to_east + to_west + to_north + to_south
    inverse = 1.0 / diagonal
    ups, downs = beside_lines(span_y, lines, folded[...])
    partial = jnp.concatenate([region[0:GY, :], region[GY : 2 * GY, :]], axis=1)
    gap = lambda rows: jnp.zeros((rows, GX), F32)
    extra = jnp.concatenate(
        [downs[3:4], gap(RY - 2), ups[0:4], gap(GY - RY - 6), downs[0:3]], axis=0
    )
    zero = (partial + extra) * (HALINE / LEVELS) * inverse

    def smooth(x):
        return inverse * (
            to_east * east_of(x) + to_west * west_of(x) + to_north * north_of(x) + to_south * south_of(x)
        )

    vectors = [zero, smooth(zero)]
    vectors.append(2.0 * smooth(vectors[1]) - vectors[0])
    vectors.append(2.0 * smooth(vectors[2]) - vectors[1])
    lane = lax.broadcasted_iota(jnp.int32, (GY, GX), 1)
    row = lax.broadcasted_iota(jnp.int32, (GY, GX), 0)
    inside = (lane < RX) & (row < RY)
    diag_out[...] = diagonal
    clean = [jnp.where(inside, v, 0.0) for v in vectors]
    position = lax.broadcasted_iota(jnp.int32, (8, 128), 1)
    packed = jnp.zeros((8, 128), F32)
    number = 0
    for i in range(4):
        basis[i] = clean[i]
        scaled = clean[i] * diagonal
        for j in range(i, 4):
            prod = scaled * clean[j]
            part = jnp.sum(prod.reshape(GY // 8, 8, GX), axis=0)
            part = part[:, 0:128] + part[:, 128:256]
            packed = packed + jnp.where(position == number, jnp.sum(part, axis=1, keepdims=True), 0.0)
            number += 1
    for d in range(dots.shape[0]):
        dots[d] = packed


def krylov_basis(span_x, span_y, region, lines, folded, extended, edges):
    return pl.pallas_call(
        functools.partial(basis_body, span_x, span_y),
        out_shape=(
            jax.ShapeDtypeStruct((4, GY, GX), F32),
            jax.ShapeDtypeStruct((GY, GX), F32),
            jax.ShapeDtypeStruct((span_x * span_y, 8, 128), F32),
            mark_shape(),
        ),
        in_specs=[vm()] * 5,
        out_specs=(vm(),) * 3 + (hbm(),),
        compiler_params=pltpu.CompilerParams(vmem_limit_bytes=12 * MIB),
        name="krylov_basis",
    )(region, lines, folded, extended, edges)


def combine_body(dots, basis, diagonal, after, height, misfit):
    sums = jnp.sum(dots[...], axis=0, keepdims=True)
    lane = lax.broadcasted_iota(jnp.int32, (1, 128), 1)
    g = {}
    number = 0
    for i in range(4):
        for j in range(i, 4):
            v = jnp.sum(jnp.where(lane == number, sums, 0.0), axis=1, keepdims=True)
            g[i, j] = g[j, i] = v
            number += 1

    def inner(a, b):
        out = jnp.zeros((1, 1), F32)
        for i in range(4):
            for j in range(4):
                if a[i] is not None and b[j] is not None:
                    out = out + a[i] * b[j] * g[i, j]
        return out

    def add(a, b):
        return a if b is None else b if a is None else a + b

    def image(a):
        out = list(a)
        for k in range(3):
            if a[k] is None:
                continue
            if k == 0:
                out[1] = add(out[1], -a[0])
            else:
                out[k + 1] = add(out[k + 1], -0.5 * a[k])
                out[k - 1] = add(out[k - 1], -0.5 * a[k])
        return out

    one = jnp.ones((1, 1), F32)
    res = [one, None, None, None]
    way = list(res)
    high = [None] * 4
    gamma = inner(res, res)
    for iteration in range(3):
        moved = image(way)
        size = gamma / inner(way, moved)
        high = [h if w is None else add(h, size * w) for h, w in zip(high, way)]
        res = [r if m is None else add(r, -size * m) for r, m in zip(res, moved)]
        if iteration < 2:
            after = inner(res, res)
            ratio = after / gamma
            way = [r if w is None else add(r, ratio * w) for r, w in zip(res, way)]
            gamma = after
    out = jnp.zeros((GY, GX), F32)
    left = jnp.zeros((GY, GX), F32)
    for k in range(4):
        v = basis[k]
        if high[k] is not None:
            out = out + high[k] * v
        left = left + res[k] * v
    gap = jnp.zeros((384 - GY, GX), F32)
    height[...] = jnp.concatenate([out, gap], axis=0).T[0:RX, 0:RY]
    misfit[...] = jnp.concatenate([left * diagonal[...], gap], axis=0).T[0:RX, 0:RY]


def combine(dots, basis, diagonal, after):
    return pl.pallas_call(
        combine_body,
        out_shape=(jax.ShapeDtypeStruct((RX, RY), F32),) * 2,
        in_specs=[vm()] * 3 + [hbm()],
        out_specs=(vm(),) * 2,
        compiler_params=pltpu.CompilerParams(vmem_limit_bytes=12 * MIB),
        name="combine",
    )(dots, basis, diagonal, after)


def across(lines):
    return lax.all_to_all(lines, "gy", split_axis=0, concat_axis=0, tiled=True)


def on_device(warm, salt, inflow, mixing, tiles, slot_depth, depth):
    span_x = lax.axis_size("gx")
    span_y = lax.axis_size("gy")
    slots = tiles.shape[0]
    cap = (KX * KY + span_x - 1) // span_x
    both = ("gx", "gy")
    bounds = [slots * i // 18 for i in (0, 12, 18)]

    def solve(part, before, after):
        first, end = bounds[part], bounds[part + 1]
        return solve_columns(warm, salt, columns, first, end - first, before, (after,))

    region_depth, lines = region_ends(span_y, depth.T)
    n_rows, q_rows, coef, pick, n_x, n_y, held = column_tables(
        span_x, span_y, mixing, tiles, slot_depth, inflow, region_depth
    )
    columns = (n_rows, q_rows, coef)
    table, extended, mark = block_edges(span_x, span_y, region_depth, across(lines), held)
    edges = lax.all_to_all(table, "gx", split_axis=0, concat_axis=0, tiled=True)
    sums = face_sums(warm, salt, columns, mark)
    flat_edges = edges.reshape(-1, EDGE)
    blocks, rows, mark = outgoing_blocks(span_x, cap, tiles, pick, flat_edges, (n_x, n_y), sums)
    got = lax.all_to_all(blocks, "gx", split_axis=0, concat_axis=0, tiled=True)
    *solved, done = solve(0, (), mark)

    region, lines, folded = region_sums(span_y, rows, got, done)
    basis, diagonal, dots, mark = krylov_basis(
        span_x, span_y, region, across(lines), folded, extended, flat_edges
    )
    sums = lax.all_to_all(dots, both, split_axis=0, concat_axis=0, tiled=True)
    *solved, done = solve(1, solved, mark)
    height, misfit = combine(sums.reshape(-1, 128), basis, diagonal, done)
    return (solved[0], solved[1], height.T, misfit.T)


def solution(mesh):
    in_specs = (
        P(("gx", "gy"), None, None),
        P(("gx", "gy"), None, None),
        P(("gx", "gy"), None),
        P(),
        P(("gx", "gy")),
        P(("gx", "gy"), None),
        P("gy", "gx"),
    )
    out_specs = (
        P(("gx", "gy"), None, None),
        P(("gx", "gy"), None, None),
        P("gy", "gx"),
        P("gy", "gx"),
    )
    return jax.shard_map(on_device, mesh=mesh, in_specs=in_specs, out_specs=out_specs, check_vma=False)
```

time: 894 us -> 71.3 us (0.08); the launches traced: 879 us -> 70.6 us
  local copies, waits for them, and re-layouts: 262 us -> 4.19 us
  blocking collectives: 200 us -> 6.71 us
  other arithmetic: 179 us -> 0 us
  waiting for transfers between devices: 179 us -> 8.55 us
  Pallas kernels: 0 us -> 33.5 us
  starting transfers between devices: 50 us -> 16.9 us
    psum x5 -> x0, blocking collectives: 200 us -> none  [the longest x3 121 us: global_sum(): return lax.psum(jnp.sum(values), ('gx', 'gy'))]
    all_to_all x2 -> x4, waiting for transfers between devices: 160 us -> 8.55 us  [the longest x1 3.36 us: on_device(): sums = lax.all_to_all(dots, both, split_axis=0, concat_axis=0, tiled=True)]
    unnamed x310 -> x12, local copies, waits for them, and re-layouts: 76.2 us -> 4.19 us
    another operation x31 -> x0, local copies, waits for them, and re-layouts: 60.8 us -> none  [weight_balanced(): return jnp.stack(layers_out, axis=1)]
    div x5 -> x0, other arithmetic: 52.9 us -> none  [the longest x2 26.2 us: thomas_vertical_inverse(): salt_rows.append(salt_term / pivots)]
    slice x21 -> x0, local copies, waits for them, and re-layouts: 51.7 us -> none  [the longest x2 25.8 us: thomas_vertical_inverse(): salt_term = saltiness_anomaly[:, stratum_position, :]]
    reduce_sum x10 -> x0, other arithmetic: 45.6 us -> none  [the longest x2 38.5 us: on_device(): jnp.sum(jnp.where(layer_index < face_levels, neighbour[:-1] - region, 0.0...]
    ppermute x28 -> x0, starting transfers between devices: 36.6 us -> none  [the longest x8 19.7 us: with_halo(): lax.ppermute(head, axis, [((i + 1) % count, i) for i in range(count)])]
  transfers between devices with their start and end apart: 30 -> 4, of which waited for: 10 -> 3; matrix products, arithmetic and copies ran while one was open for 35% -> 0% of each run, Pallas kernels for 0% -> 35%
where the time goes in v1:
time: 71.3 us; the launch traced here: 70.6 us
  Pallas kernels  33.5 us (47%)
  starting transfers between devices  16.9 us (24%)
  waiting for transfers between devices  8.55 us (12%)
  blocking collectives  6.71 us (9%)
  local copies, waits for them, and re-layouts  4.19 us (6%)
    pallas_call x2, Pallas kernels, solve_columns(): pl.pallas_call(functools.partial(solve_body, first, group, extra), grid=(...  14 us
    pallas_call x1, Pallas kernels, face_sums(): pl.pallas_call(functools.partial(flux_body, slots, group), grid=(slots //...  9.89 us
    all_to_all x1, blocking collectives, across(): return lax.all_to_all(lines, 'gy', split_axis=0, concat_axis=0, tiled=True)  6.71 us
    all_to_all x1, starting transfers between devices, on_device(): edges = lax.all_to_all(table, 'gx', split_axis=0, concat_axis=0, tiled=True)  6.29 us
    all_to_all x1, starting transfers between devices, across(): return lax.all_to_all(lines, 'gy', split_axis=0, concat_axis=0, tiled=True)  4.24 us
    unnamed x12, local copies, waits for them, and re-layouts  4.19 us
    all_to_all x1, starting transfers between devices, on_device(): got = lax.all_to_all(blocks, 'gx', split_axis=0, concat_axis=0, tiled=True)  3.63 us
    all_to_all x1, waiting for transfers between devices, on_device(): sums = lax.all_to_all(dots, both, split_axis=0, concat_axis=0, tiled=True)  3.36 us
  transfers between devices with their start and end apart: 4, of which 3 were waited for; matrix products, arithmetic and copies ran while one was open for 0% of the time, Pallas kernels for 35%

profile of v1, /device:TPU:0, one launch (start us, length us, event | category | flops | bytes accessed | tf_op | source)
XLA Modules:
  0.0 70.6 jit_solution(8661288530807660189)
XLA Ops:
  0.6 0.0 copy-start.2
  0.6 0.9 %copy-done.2 = s32[300,180]{0,1:T(8,128)S(1)} copy-done((s32[300,180]{0,1:T(8,128)S(1)}, s32[300,180]{0,1:T(8,128)}, u32[]{:S(2)}) %copy-start.2) | copy-done | bytes 216024
  1.6 0.8 %region_ends.1 = (f32[312,256]{1,0:T(8,128)S(1)}, f32[4,8,256]{2,1,0:T(8,128)}) custom-call(s32[180,300]{1,0:T(8,128)S(1)} %bitcast.10), custom_call_target="tpu_custom_call" | custom-call | tf_op jit(solution)/shard_map/region_ends/pallas_call | solution.py:369
  2.4 4.2 %all-to-all-start = ((f32[4,8,256]{2,1,0:T(8,128)}), f32[4,8,256]{2,1,0:T(8,128)S(1)}, u32[]{:S(2)}, u32[]{:S(2)}) async-start(f32[4,8,256]{2,1,0:T(8,128)} %get-tuple-element.42), calls=%async_computation | async-start | bytes 65536 | tf_op jit(solution)/shard_map/all_to_all | solution.py:961
  6.6 0.0 copy-start
  6.6 1.0 %copy-done = s32[18,3000]{1,0:T(8,128)S(1)} copy-done((s32[18,3000]{1,0:T(8,128)S(1)}, s32[18,3000]{1,0:T(8,128)}, u32[]{:S(2)}) %copy-start) | copy-done | bytes 216024
  7.6 0.0 copy-start.1
  7.6 1.0 %copy-done.1 = f32[18,3000]{1,0:T(8,128)S(1)} copy-done((f32[18,3000]{1,0:T(8,128)S(1)}, f32[18,3000]{1,0:T(8,128)}, u32[]{:S(2)}) %copy-start.1) | copy-done | bytes 216024
  8.5 0.0 copy-start.3
  8.5 0.7 copy-done.3
  9.2 0.0 copy-start.5
  9.2 0.7 copy-done.5
  9.8 0.9 %column_tables.1 = (s32[608,128]{1,0:T(8,128)S(1)}, f32[608,128]{1,0:T(8,128)S(1)}, f32[720,128]{1,0:T(8,128)S(1)}, f32[96,256]{1,0:T(8,128)S(1)}, f32[24,128]{1...) custom-call(f32[29]{0:T(128)S(1)} %copy-done.5, s32[18]{0:T(128)S(1)} %copy-done.3, s32[18,3000]{1,0:T(8,128)S(1)} %copy-done, ...), custom_call_target="tpu_custom_call" | custom-call | flops 5000000 | bytes 3000000 | tf_op jit(solution)/shard_map/column_tables/pallas_call | solution.py:261
  10.8 0.0 all-to-all-done.lines
  10.8 1.0 %block_edges.1 = (f32[8,32,384]{2,1,0:T(8,128)}, f32[312,256]{1,0:T(8,128)S(1)}, f32[8,128]{1,0:T(8,128)S(1)}) custom-call(f32[312,256]{1,0:T(8,128)S(1)} %get-tuple-element.37.after.depth, f32[4,8,256]{2,1,0:T(8,128)S(1)} %all-to-all-done.lines, f32[8,128]{1,0:T(8,128)S(1)} %get-tuple-element.43.held), custom_call_target="tpu_custom_call" | custom-call | tf_op jit(solution)/shard_map/block_edges/pallas_call | solution.py:342
  11.8 6.3 %all-to-all-start.1 = ((f32[8,32,384]{2,1,0:T(8,128)}), f32[8,32,384]{2,1,0:T(8,128)S(1)}, u32[]{:S(2)}, u32[]{:S(2)}) async-start(f32[8,32,384]{2,1,0:T(8,128)} %get-tuple-element.44), calls=%async_computation.1 | async-start | bytes 786432 | tf_op jit(solution)/shard_map/all_to_all | solution.py:982
  18.1 0.0 copy-start.4
  18.1 9.9 %face_sums.1 = (f32[656,128]{1,0:T(8,128)S(1)}, f32[18,32,128]{2,1,0:T(8,128)S(1)}, f32[18,32,128]{2,1,0:T(8,128)S(1)}) custom-call(f32[18,30,3000]{2,1,0:T(8,128)} %warm.5, f32[18,30,3000]{2,1,0:T(8,128)} %salt.5, s32[608,128]{1,0:T(8,128)S(1)} %get-tuple-element.38.n_rows, f32[608,128]{1,0:T(8,128)S(1)} %get-tuple-element.39.q_rows, ...), custom_call_target="tpu_custom_call" | custom-call | flops 40000000 | bytes 15000000 | tf_op jit(solution)/shard_map/face_sums/pallas_call | solution.py:520
  28.0 2.4 %all-to-all-done.1 = f32[8,32,384]{2,1,0:T(8,128)S(1)} async-done(((f32[8,32,384]{2,1,0:T(8,128)}), f32[8,32,384]{2,1,0:T(8,128)S(1)}, u32[]{:S(2)}, u32[]{:S(2)}) %all-to-all-start.1) | async-done | bytes 393248 | tf_op jit(solution)/shard_map/all_to_all | solution.py:982
  30.4 0.0 copy-done.4
  30.4 2.2 %outgoing_blocks.1 = (f32[24,32,128]{2,1,0:T(8,128)}, s32[40,128]{1,0:T(8,128)S(1)}, f32[8,128]{1,0:T(8,128)S(1)}) custom-call(s32[18]{0:T(128)S(1)} %copy-done.4, f32[96,256]{1,0:T(8,128)S(1)} %get-tuple-element.41.pick, f32[256,384]{1,0:T(8,128)S(1)} %bitcast.6, f32[24,128]{1,0:T(8,128)S(1)} %get-tuple-element.45.n_x, ...), custom_call_target="tpu_custom_call" | custom-call | tf_op jit(solution)/shard_map/outgoing_blocks/pallas_call | solution.py:670
  32.6 3.6 %all-to-all-start.2 = ((f32[24,32,128]{2,1,0:T(8,128)}), f32[24,32,128]{2,1,0:T(8,128)S(1)}, u32[]{:S(2)}, u32[]{:S(2)}) async-start(f32[24,32,128]{2,1,0:T(8,128)} %get-tuple-element.55), calls=%async_computation.2 | async-start | bytes 786432 | tf_op jit(solution)/shard_map/all_to_all | solution.py:986
  36.2 9.1 %column_solve.2 = (f32[18,30,3000]{2,1,0:T(8,128)}, f32[18,30,3000]{2,1,0:T(8,128)}, f32[8,128]{1,0:T(8,128)S(1)}) custom-call(f32[18,30,3000]{2,1,0:T(8,128)} %warm.5, f32[18,30,3000]{2,1,0:T(8,128)} %salt.5, s32[608,128]{1,0:T(8,128)S(1)} %get-tuple-element.38.n_rows, f32[608,128]{1,0:T(8,128)S(1)} %get-tuple-element.39.q_rows, ...), custom_call_target="tpu_custom_call" | custom-call | flops 24000000 | bytes 19200000 | tf_op jit(solution)/shard_map/column_solve/pallas_call | solution.py:169
  45.3 2.8 %all-to-all-done.2 = f32[24,32,128]{2,1,0:T(8,128)S(1)} async-done(((f32[24,32,128]{2,1,0:T(8,128)}), f32[24,32,128]{2,1,0:T(8,128)S(1)}, u32[]{:S(2)}, u32[]{:S(2)}) %all-to-all-start.2) | async-done | bytes 393248 | tf_op jit(solution)/shard_map/all_to_all | solution.py:986
  48.1 1.4 %region_sums.1 = (f32[624,128]{1,0:T(8,128)S(1)}, f32[4,8,256]{2,1,0:T(8,128)S(1)}, f32[8,256]{1,0:T(8,128)S(1)}) custom-call(s32[40,128]{1,0:T(8,128)S(1)} %get-tuple-element.54.rows, f32[768,128]{1,0:T(8,128)S(1)} %bitcast.8, f32[8,128]{1,0:T(8,128)S(1)} %get-tuple-element.56.after), custom_call_target="tpu_custom_call" | custom-call | tf_op jit(solution)/shard_map/region_sums/pallas_call | solution.py:777
  49.5 6.7 %all_to_all.25.lines = f32[4,8,256]{2,1,0:T(8,128)S(1)} all-to-all(f32[4,8,256]{2,1,0:T(8,128)S(1)} %get-tuple-element.58), channel_id=1, replica_groups=mesh['gx'=8,'gy'=4] {'gy'}, dimensions={0} | all-to-all | bytes 65536 | tf_op jit(solution)/shard_map/all_to_all | solution.py:961
  56.2 2.2 %krylov_basis.1 = (f32[4,312,256]{2,1,0:T(8,128)S(1)}, f32[312,256]{1,0:T(8,128)S(1)}, f32[32,8,128]{2,1,0:T(8,128)}, f32[8,128]{1,0:T(8,128)S(1)}) custom-call(f32[624,128]{1,0:T(8,128)S(1)} %get-tuple-element.57.region, f32[4,8,256]{2,1,0:T(8,128)S(1)} %all_to_all.25.lines, f32[8,256]{1,0:T(8,128)S(1)} %get-tuple-element.59.folded, ...), custom_call_target="tpu_custom_call" | custom-call | tf_op jit(solution)/shard_map/krylov_basis/pallas_call | solution.py:873
  58.4 2.7 %all-to-all-start.4 = ((f32[32,8,128]{2,1,0:T(8,128)}), f32[32,8,128]{2,1,0:T(8,128)S(1)}, u32[]{:S(2)}, u32[]{:S(2)}) async-start(f32[32,8,128]{2,1,0:T(8,128)} %get-tuple-element.64), calls=%async_computation.4 | async-start | bytes 262144 | tf_op jit(solution)/shard_map/all_to_all | solution.py:993
  61.1 4.9 %column_solve.3 = (f32[18,30,3000]{2,1,0:T(8,128)}, f32[18,30,3000]{2,1,0:T(8,128)}, f32[8,128]{1,0:T(8,128)S(1)}) custom-call(f32[18,30,3000]{2,1,0:T(8,128)} %warm.5, f32[18,30,3000]{2,1,0:T(8,128)} %salt.5, s32[608,128]{1,0:T(8,128)S(1)} %get-tuple-element.38.n_rows, ...), custom_call_target="tpu_custom_call", output_to_operand_aliasing={{0}: (5, {}), {1}: (6, {})} | custom-call | flops 12000000 | bytes 9600000 | tf_op jit(solution)/shard_map/column_solve/pallas_call | solution.py:169
  66.0 3.4 %all-to-all-done.4 = f32[32,8,128]{2,1,0:T(8,128)S(1)} async-done(((f32[32,8,128]{2,1,0:T(8,128)}), f32[32,8,128]{2,1,0:T(8,128)S(1)}, u32[]{:S(2)}, u32[]{:S(2)}) %all-to-all-start.4) | async-done | bytes 131104 | tf_op jit(solution)/shard_map/all_to_all | solution.py:993
  69.4 1.2 %combine.1 = (f32[180,300]{1,0:T(8,128)}, f32[180,300]{1,0:T(8,128)}) custom-call(f32[256,128]{1,0:T(8,128)S(1)} %bitcast.9, f32[4,312,256]{2,1,0:T(8,128)S(1)} %get-tuple-element.65.basis, f32[312,256]{1,0:T(8,128)S(1)} %get-tuple-element.66.diagonal, f32[8,128]{1,0:T(8,128)S(1)} %get-tuple-element.67.after), custom_call_target="tpu_custom_call" | custom-call | tf_op jit(solution)/shard_map/combine/pallas_call | solution.py:950
Async XLA Ops:
  0.6 1.0 %copy-start.2 = (s32[300,180]{0,1:T(8,128)S(1)}, s32[300,180]{0,1:T(8,128)}, u32[]{:S(2)}) copy-start(s32[300,180]{0,1:T(8,128)} %param.13) | copy-start | bytes 648004
  2.4 8.4 %all-to-all-start = ((f32[4,8,256]{2,1,0:T(8,128)}), f32[4,8,256]{2,1,0:T(8,128)S(1)}, u32[]{:S(2)}, u32[]{:S(2)}) async-start(f32[4,8,256]{2,1,0:T(8,128)} %get-tuple-element.42), calls=%async_computation | async-start | bytes 65536 | tf_op jit(solution)/shard_map/all_to_all | solution.py:961
  6.6 1.0 %copy-start = (s32[18,3000]{1,0:T(8,128)S(1)}, s32[18,3000]{1,0:T(8,128)}, u32[]{:S(2)}) copy-start(s32[18,3000]{1,0:T(8,128)} %depth.1) | copy-start | bytes 648004
  7.6 1.0 %copy-start.1 = (f32[18,3000]{1,0:T(8,128)S(1)}, f32[18,3000]{1,0:T(8,128)}, u32[]{:S(2)}) copy-start(f32[18,3000]{1,0:T(8,128)} %inflow.1) | copy-start | bytes 648004
  8.5 0.7 copy-start.3
  9.2 0.7 copy-start.5
  11.8 18.6 %all-to-all-start.1 = ((f32[8,32,384]{2,1,0:T(8,128)}), f32[8,32,384]{2,1,0:T(8,128)S(1)}, u32[]{:S(2)}, u32[]{:S(2)}) async-start(f32[8,32,384]{2,1,0:T(8,128)} %get-tuple-element.44), calls=%async_computation.1 | async-start | bytes 786432 | tf_op jit(solution)/shard_map/all_to_all | solution.py:982
  18.1 12.3 %copy-start.4 = (s32[18]{0:T(128)S(1)}, s32[18]{0:T(128)}, u32[]{:S(2)}) copy-start(s32[18]{0:T(128)} %ids.3) | copy-start | bytes 220
  32.6 15.5 %all-to-all-start.2 = ((f32[24,32,128]{2,1,0:T(8,128)}), f32[24,32,128]{2,1,0:T(8,128)S(1)}, u32[]{:S(2)}, u32[]{:S(2)}) async-start(f32[24,32,128]{2,1,0:T(8,128)} %get-tuple-element.55), calls=%async_computation.2 | async-start | bytes 786432 | tf_op jit(solution)/shard_map/all_to_all | solution.py:986
  58.4 11.0 %all-to-all-start.4 = ((f32[32,8,128]{2,1,0:T(8,128)}), f32[32,8,128]{2,1,0:T(8,128)S(1)}, u32[]{:S(2)}, u32[]{:S(2)}) async-start(f32[32,8,128]{2,1,0:T(8,128)} %get-tuple-element.64), calls=%async_computation.4 | async-start | bytes 262144 | tf_op jit(solution)/shard_map/all_to_all | solution.py:993

commit v2 on v1

--- a/solution.py
+++ b/solution.py
@@ -100,58 +100,102 @@
     return pl.ds(j * ROW_SIZE + u * 8 * PITCH + k, 8, stride=PITCH)
 
 
-def solve_body(first, group, extra, warm, salt, n_rows, q_rows, coef, *rest):
-    warm_out, salt_out, _, warm_rows, salt_rows, warm_mid, salt_mid = rest[extra:]
-    step = pl.program_id(0)
-    many = range(group)
-    each = [(j, u) for j in many for u in range(TILES // 8)]
-    n, t, s = {}, {}, {}
-    for j in many:
-        copy_in(warm_rows, j * ROW_SIZE, lambda c, w: warm[j, :, c * 128 : c * 128 + w])
-        copy_in(salt_rows, j * ROW_SIZE, lambda c, w: salt[j, :, c * 128 : c * 128 + w])
-        slot = first + step * group + j
-        for u, deep in enumerate(pieces_of(n_rows, slot, STEP)):
-            n[j, u] = deep
-        for u, heat in enumerate(pieces_of(q_rows, slot, STEP)):
-            t[j, u] = jnp.where(n[j, u] > 0, heat, 0.0)
-    for k in range(LEVELS):
-        g = coefficient(coef, 0, k - 1) if k else None
-        for j, u in each:
-            rt = warm_rows[columns_at(j, k, u), :]
-            rs = salt_rows[columns_at(j, k, u), :]
-            if k == 0:
-                t[j, u] = rt + t[j, u]
-                s[j, u] = rs
-            else:
-                e = jnp.where(n[j, u] > k, g, 0.0)
-                t[j, u] = rt + e * t[j, u]
-                s[j, u] = rs + e * s[j, u]
-            warm_mid[level_at(j, k, u), :] = t[j, u]
-            salt_mid[level_at(j, k, u), :] = s[j, u]
-    for k in range(LEVELS - 1, -1, -1):
-        last = coefficient(coef, 2, k)
-        q = coefficient(coef, 1, k) if k + 1 < LEVELS else None
-        g = coefficient(coef, 0, k) if k + 1 < LEVELS else None
-        for j, u in each:
-            a = jnp.where(n[j, u] > k, last, 1.0)
-            if k + 1 < LEVELS:
-                more = n[j, u] > k + 1
-                a = jnp.where(more, q, a)
-                e = jnp.where(more, g, 0.0)
-                t[j, u] = a * warm_mid[level_at(j, k, u), :] + e * t[j, u]
-                s[j, u] = a * salt_mid[level_at(j, k, u), :] + e * s[j, u]
-            else:
-                t[j, u] = a * t[j, u]
-                s[j, u] = a * s[j, u]
-            warm_mid[level_at(j, k, u), :] = t[j, u]
-            salt_mid[level_at(j, k, u), :] = s[j, u]
-    for j in many:
+AHEAD = 4
+BEHIND = 3
+
+
+def solve_body(first, count, extra, warm, salt, n_rows, q_rows, coef, *rest):
+    warm_out, salt_out, _, warm_in, salt_in, warm_done, salt_done, *rest = rest[extra:]
+    warm_rows, salt_rows, warm_mid, salt_mid, came, left = rest
+
+    def fetch(i):
+        b = lax.rem(i, AHEAD)
+        return [
+            pltpu.make_async_copy(source.at[first + i], to.at[b], came.at[b, d])
+            for d, (source, to) in enumerate(((warm, warm_in), (salt, salt_in)))
+        ]
+
+    def put(i):
+        b = lax.rem(i, BEHIND)
+        return [
+            pltpu.make_async_copy(source.at[b], to.at[first + i], left.at[b, d])
+            for d, (source, to) in enumerate(((warm_done, warm_out), (salt_done, salt_out)))
+        ]
+
+    for i in range(min(AHEAD, count)):
+        for copy in fetch(i):
+            copy.start()
+    each = [(0, u) for u in range(TILES // 8)]
+
+    def one(i, carry):
+        b = lax.rem(i, AHEAD)
+        n, t, s = {}, {}, {}
+        for copy in fetch(i):
+            copy.wait()
+        copy_in(warm_rows, 0, lambda c, w: warm_in[b, :, c * 128 : c * 128 + w])
+        copy_in(salt_rows, 0, lambda c, w: salt_in[b, :, c * 128 : c * 128 + w])
+
+        @pl.when(i + AHEAD < count)
+        def _():
+            for copy in fetch(i + AHEAD):
+                copy.start()
+
+        for u, deep in enumerate(pieces_of(n_rows, first + i, STEP)):
+            n[0, u] = deep
+        for u, heat in enumerate(pieces_of(q_rows, first + i, STEP)):
+            t[0, u] = jnp.where(n[0, u] > 0, heat, 0.0)
+        for k in range(LEVELS):
+            g = coefficient(coef, 0, k - 1) if k else None
+            for j, u in each:
+                rt = warm_rows[columns_at(j, k, u), :]
+                rs = salt_rows[columns_at(j, k, u), :]
+                if k == 0:
+                    t[j, u] = rt + t[j, u]
+                    s[j, u] = rs
+                else:
+                    e = jnp.where(n[j, u] > k, g, 0.0)
+                    t[j, u] = rt + e * t[j, u]
+                    s[j, u] = rs + e * s[j, u]
+                warm_mid[level_at(j, k, u), :] = t[j, u]
+                salt_mid[level_at(j, k, u), :] = s[j, u]
+        for k in range(LEVELS - 1, -1, -1):
+            last = coefficient(coef, 2, k)
+            q = coefficient(coef, 1, k) if k + 1 < LEVELS else None
+            g = coefficient(coef, 0, k) if k + 1 < LEVELS else None
+            for j, u in each:
+                a = jnp.where(n[j, u] > k, last, 1.0)
+                if k + 1 < LEVELS:
+                    more = n[j, u] > k + 1
+                    a = jnp.where(more, q, a)
+                    e = jnp.where(more, g, 0.0)
+                    t[j, u] = a * warm_mid[level_at(j, k, u), :] + e * t[j, u]
+                    s[j, u] = a * salt_mid[level_at(j, k, u), :] + e * s[j, u]
+                else:
+                    t[j, u] = a * t[j, u]
+                    s[j, u] = a * s[j, u]
+                warm_mid[level_at(j, k, u), :] = t[j, u]
+                salt_mid[level_at(j, k, u), :] = s[j, u]
+
+        @pl.when(i >= BEHIND)
+        def _():
+            for copy in put(i - BEHIND):
+                copy.wait()
+
+        o = lax.rem(i, BEHIND)
         for c, w in widths():
             for k in range(0, LEVELS, 8):
                 h = min(8, LEVELS - k)
-                part = pl.ds(j * MID_SIZE + k * MID + c, h, stride=MID)
-                warm_out[j, k : k + h, c * 128 : c * 128 + w] = warm_mid[part, :][:, 0:w]
-                salt_out[j, k : k + h, c * 128 : c * 128 + w] = salt_mid[part, :][:, 0:w]
+                part = pl.ds(k * MID + c, h, stride=MID)
+                warm_done[o, k : k + h, c * 128 : c * 128 + w] = warm_mid[part, :][:, 0:w]
+                salt_done[o, k : k + h, c * 128 : c * 128 + w] = salt_mid[part, :][:, 0:w]
+        for copy in put(i):
+            copy.start()
+        return carry
+
+    lax.fori_loop(0, count, one, 0)
+    for i in range(max(0, count - BEHIND), count):
+        for copy in put(i):
+            copy.wait()
 
 
 def mark_shape():
@@ -163,21 +207,18 @@
 
 
 def solve_columns(warm, salt, columns, first, count, before, after):
-    group = 3 if first % 3 == 0 and count % 3 == 0 else 1
-    block = pl.BlockSpec((group, LEVELS, COLS), lambda i: (first // group + i, 0, 0))
     extra = len(before) + len(after)
+    blocks = lambda size: pltpu.VMEM((size, LEVELS, COLS), F32)
     return pl.pallas_call(
-        functools.partial(solve_body, first, group, extra),
-        grid=(count // group,),
+        functools.partial(solve_body, first, count, extra),
         out_shape=(jax.ShapeDtypeStruct(warm.shape, F32), jax.ShapeDtypeStruct(salt.shape, F32), mark_shape()),
-        in_specs=[block, block] + [vm()] * 3 + [hbm()] * extra,
-        out_specs=(block, block, hbm()),
-        scratch_shapes=[
-            pltpu.VMEM((group * ROW_SIZE, 128), F32),
-            pltpu.VMEM((group * ROW_SIZE, 128), F32),
-            pltpu.VMEM((group * MID_SIZE, 128), F32),
-            pltpu.VMEM((group * MID_SIZE, 128), F32),
-        ],
+        in_specs=[hbm(), hbm()] + [vm()] * 3 + [hbm()] * extra,
+        out_specs=(hbm(), hbm(), hbm()),
+        scratch_shapes=[blocks(AHEAD)] * 2
+        + [blocks(BEHIND)] * 2
+        + [pltpu.VMEM((ROW_SIZE, 128), F32)] * 2
+        + [pltpu.VMEM((MID_SIZE, 128), F32)] * 2
+        + [pltpu.SemaphoreType.DMA((AHEAD, 2)), pltpu.SemaphoreType.DMA((BEHIND, 2))],
         input_output_aliases={5: 0, 6: 1} if before else {},
         compiler_params=pltpu.CompilerParams(vmem_limit_bytes=49 * MIB),
         cost_estimate=pl.CostEstimate(flops=count * 2_000_000, bytes_accessed=count * 1_600_000, transcendentals=0),
@@ -397,139 +438,158 @@
 
 def flux_body(
     slots, group, warm, salt, n_rows, q_rows, coef, after, pieces, rim_x, rim_y,
-    faces, found, rows, middle, totals,
+    faces, found, rows, middle, totals, warm_in, salt_in, came,
 ):
-    step = pl.program_id(0)
     lane = lax.broadcasted_iota(jnp.int32, (1, FLAT), 1)
     col = lane - SPAN_E * divide(lane, SPAN_E)
 
-    @pl.when(step == 0)
-    def _():
-        faces[...] = jnp.zeros(faces.shape, jnp.int32)
-
-    many = range(group)
-    each = [(j, u) for j in many for u in range(TILES // 8)]
-    place = lax.broadcasted_iota(jnp.int32, (TILES, 128), 0) * 128
-    place = place + lax.broadcasted_iota(jnp.int32, (TILES, 128), 1)
-    in_row = place - SPAN_E * divide(place, SPAN_E)
-    n, x = {}, {}
-    for j in many:
-        copy_in(
-            rows,
-            j * ROW_SIZE,
-            lambda c, w: salt[j, :, c * 128 : c * 128 + w] - RATIO * warm[j, :, c * 128 : c * 128 + w],
+    def fetch(step):
+        b = lax.rem(step, 2) * group
+        return [
+            pltpu.make_async_copy(source.at[step * group + j], to.at[b + j], came.at[b + j, d])
+            for j in range(group)
+            for d, (source, to) in enumerate(((warm, warm_in), (salt, salt_in)))
+        ]
+
+    for step in range(min(2, slots // group)):
+        for copy in fetch(step):
+            copy.start()
+    faces[...] = jnp.zeros(faces.shape, jnp.int32)
+
+    def one(step, carry):
+        b = lax.rem(step, 2) * group
+        many = range(group)
+        each = [(j, u) for j in many for u in range(TILES // 8)]
+        place = lax.broadcasted_iota(jnp.int32, (TILES, 128), 0) * 128
+        place = place + lax.broadcasted_iota(jnp.int32, (TILES, 128), 1)
+        in_row = place - SPAN_E * divide(place, SPAN_E)
+        n, x = {}, {}
+        for copy in fetch(step):
+            copy.wait()
+        for j in many:
+            copy_in(
+                rows,
+                j * ROW_SIZE,
+                lambda c, w: salt_in[b + j, :, c * 128 : c * 128 + w] - RATIO * warm_in[b + j, :, c * 128 : c * 128 + w],
+            )
+            slot = step * group + j
+            for u, deep in enumerate(pieces_of(n_rows, slot, STEP)):
+                n[j, u] = deep
+            for u, heat in enumerate(pieces_of(q_rows, slot, STEP)):
+                x[j, u] = RATIO * heat
+            deep = jnp.concatenate([n[j, u] for u in range(TILES // 8)], axis=0)
+            for d, (by, inside) in enumerate(
+                (
+                    (1, in_row < SPAN_E - 1),
+                    (-1, in_row > 0),
+                    (SPAN_E, place < COLS - SPAN_E),
+                    (-SPAN_E, place >= SPAN_E),
+                )
+            ):
+                start = (8 * j + d) * MID
+                faces[start : start + TILES, :] = jnp.where(inside, jnp.minimum(deep, shifted(deep, by)), 0)
+
+        @pl.when(step + 2 < slots // group)
+        def _():
+            for copy in fetch(step + 2):
+                copy.start()
+
+        for k in range(LEVELS):
+            g = coefficient(coef, 0, k - 1) if k else None
+            for j, u in each:
+                right = rows[columns_at(j, k, u), :]
+                x[j, u] = right + g * x[j, u] if k else right - x[j, u]
+                middle[j, k, u * 8 : u * 8 + 8, :] = x[j, u]
+        for k in range(LEVELS - 1, -1, -1):
+            last = coefficient(coef, 2, k)
+            q = coefficient(coef, 1, k) if k + 1 < LEVELS else None
+            g = coefficient(coef, 0, k) if k + 1 < LEVELS else None
+            for j, u in each:
+                if k + 1 < LEVELS:
+                    more = n[j, u] > k + 1
+                    a = jnp.where(more, q, last)
+                    e = jnp.where(more, g, 0.0)
+                    x[j, u] = a * middle[j, k, u * 8 : u * 8 + 8, :] + e * x[j, u]
+                else:
+                    x[j, u] = last * x[j, u]
+                middle[j, k, u * 8 : u * 8 + 8, :] = x[j, u]
+        zero = jnp.zeros((8, 128), F32)
+        pressure = {at: zero for at in each}
+        total = {at: zero for at in each}
+        for k in range(LEVELS):
+            for j, u in each:
+                pressure[j, u] = pressure[j, u] + middle[j, k, u * 8 : u * 8 + 8, :]
+                total[j, u] = total[j, u] + pressure[j, u]
+                totals[level_at(j, k, u), :] = total[j, u]
+
+        for j in many:
+            slot = step * group + j
+
+            def tile(c):
+                now = [totals[pl.ds(j * MID_SIZE + 8 * g * MID + c, 8, stride=MID), :] for g in range(4)]
+                level = faces[pl.ds(8 * j * MID + c, 8, stride=MID), :] - 1
+                sums = zero
+                for g in range(4):
+                    one_of = jnp.take_along_axis(now[g], level & 7, axis=0, mode="promise_in_bounds")
+                    sums = jnp.where((level >> 3) == g, one_of, sums)
+                found[pl.ds(slot * SLOT_STEP + c * 8, 8), :] = sums
+                return now
+
+            for ref, parts in zip((rim_x, rim_y), rim_of(tile)):
+                for g in range(4):
+                    ref[slot, 8 * g : 8 * g + 8, :] = parts[g]
+        return carry
+
+    lax.fori_loop(0, slots // group, one, 0)
+
+    def flat(d):
+        return jnp.concatenate(
+            [found[pl.ds(c * 8 + d, SLOT_ROWS, stride=SLOT_STEP), :] for c in range(TILES)], axis=1
         )
-        slot = step * group + j
-        for u, deep in enumerate(pieces_of(n_rows, slot, STEP)):
-            n[j, u] = deep
-        for u, heat in enumerate(pieces_of(q_rows, slot, STEP)):
-            x[j, u] = RATIO * heat
-        deep = jnp.concatenate([n[j, u] for u in range(TILES // 8)], axis=0)
-        for d, (by, inside) in enumerate(
-            (
-                (1, in_row < SPAN_E - 1),
-                (-1, in_row > 0),
-                (SPAN_E, place < COLS - SPAN_E),
-                (-SPAN_E, place >= SPAN_E),
-            )
-        ):
-            start = (8 * j + d) * MID
-            faces[start : start + TILES, :] = jnp.where(inside, jnp.minimum(deep, shifted(deep, by)), 0)
-    for k in range(LEVELS):
-        g = coefficient(coef, 0, k - 1) if k else None
-        for j, u in each:
-            right = rows[columns_at(j, k, u), :]
-            x[j, u] = right + g * x[j, u] if k else right - x[j, u]
-            middle[j, k, u * 8 : u * 8 + 8, :] = x[j, u]
-    for k in range(LEVELS - 1, -1, -1):
-        last = coefficient(coef, 2, k)
-        q = coefficient(coef, 1, k) if k + 1 < LEVELS else None
-        g = coefficient(coef, 0, k) if k + 1 < LEVELS else None
-        for j, u in each:
-            if k + 1 < LEVELS:
-                more = n[j, u] > k + 1
-                a = jnp.where(more, q, last)
-                e = jnp.where(more, g, 0.0)
-                x[j, u] = a * middle[j, k, u * 8 : u * 8 + 8, :] + e * x[j, u]
-            else:
-                x[j, u] = last * x[j, u]
-            middle[j, k, u * 8 : u * 8 + 8, :] = x[j, u]
-    zero = jnp.zeros((8, 128), F32)
-    pressure = {at: zero for at in each}
-    total = {at: zero for at in each}
-    for k in range(LEVELS):
-        for j, u in each:
-            pressure[j, u] = pressure[j, u] + middle[j, k, u * 8 : u * 8 + 8, :]
-            total[j, u] = total[j, u] + pressure[j, u]
-            totals[level_at(j, k, u), :] = total[j, u]
-
-    for j in many:
-        slot = step * group + j
-
-        def tile(c):
-            now = [totals[pl.ds(j * MID_SIZE + 8 * g * MID + c, 8, stride=MID), :] for g in range(4)]
-            level = faces[pl.ds(8 * j * MID + c, 8, stride=MID), :] - 1
-            sums = zero
-            for g in range(4):
-                one_of = jnp.take_along_axis(now[g], level & 7, axis=0, mode="promise_in_bounds")
-                sums = jnp.where((level >> 3) == g, one_of, sums)
-            found[pl.ds(slot * SLOT_STEP + c * 8, 8), :] = sums
-            return now
-
-        for ref, parts in zip((rim_x, rim_y), rim_of(tile)):
-            for g in range(4):
-                ref[j, 8 * g : 8 * g + 8, :] = parts[g]
-
-    @pl.when(step == slots // group - 1)
-    def _():
-        def flat(d):
-            return jnp.concatenate(
-                [found[pl.ds(c * 8 + d, SLOT_ROWS, stride=SLOT_STEP), :] for c in range(TILES)], axis=1
-            )
-
-        east, west, north, south = (flat(d) for d in range(4))
-        from_east = pltpu.roll(west, FLAT - 1, 1)
-        from_west = pltpu.roll(east, 1, 1)
-        net = -(east + west + north + south)
-        net = net + jnp.where(col < SPAN_E - 1, from_east, 0.0)
-        net = net + jnp.where(col > 0, from_west, 0.0)
-        net = net + jnp.where(lane < COLS - SPAN_E, pltpu.roll(south, FLAT - SPAN_E, 1), 0.0)
-        net = net + jnp.where(lane >= SPAN_E, pltpu.roll(north, SPAN_E, 1), 0.0)
-        l = lax.broadcasted_iota(jnp.int32, (1, 128), 1)
-        for t in range(26):
-            halves = []
-            for h in range(2):
-                r = 2 * t + h
-                if r in (0, SPAN_N + 1):
-                    continue
-                start = (r - 1) * SPAN_E
-                a = start // 128
-                row = net[:, a * 128 : a * 128 + 128]
-                if start % 128 + SPAN_E > 128:
-                    row = jnp.where(l >= start % 128, row, net[:, a * 128 + 128 : a * 128 + 256])
-                row = pltpu.roll(row, (64 * h + 1 - start) % 128, 1)
-                halves.append(jnp.where((l > 64 * h) & (l <= 64 * h + SPAN_E), row, 0.0))
-            pieces[t * STEP : t * STEP + SLOT_ROWS, :] = halves[0] + halves[1] if len(halves) == 2 else halves[0]
+
+    east, west, north, south = (flat(d) for d in range(4))
+    from_east = pltpu.roll(west, FLAT - 1, 1)
+    from_west = pltpu.roll(east, 1, 1)
+    net = -(east + west + north + south)
+    net = net + jnp.where(col < SPAN_E - 1, from_east, 0.0)
+    net = net + jnp.where(col > 0, from_west, 0.0)
+    net = net + jnp.where(lane < COLS - SPAN_E, pltpu.roll(south, FLAT - SPAN_E, 1), 0.0)
+    net = net + jnp.where(lane >= SPAN_E, pltpu.roll(north, SPAN_E, 1), 0.0)
+    l = lax.broadcasted_iota(jnp.int32, (1, 128), 1)
+    for t in range(26):
+        halves = []
+        for h in range(2):
+            r = 2 * t + h
+            if r in (0, SPAN_N + 1):
+                continue
+            start = (r - 1) * SPAN_E
+            a = start // 128
+            row = net[:, a * 128 : a * 128 + 128]
+            if start % 128 + SPAN_E > 128:
+                row = jnp.where(l >= start % 128, row, net[:, a * 128 + 128 : a * 128 + 256])
+            row = pltpu.roll(row, (64 * h + 1 - start) % 128, 1)
+            halves.append(jnp.where((l > 64 * h) & (l <= 64 * h + SPAN_E), row, 0.0))
+        pieces[t * STEP : t * STEP + SLOT_ROWS, :] = halves[0] + halves[1] if len(halves) == 2 else halves[0]
 
 
 def face_sums(warm, salt, columns, after):
     slots = warm.shape[0]
     group = 3 if slots % 3 == 0 else 1
-    block = pl.BlockSpec((group, LEVELS, COLS), lambda i: (i, 0, 0))
-    rim = pl.BlockSpec((group, 32, 128), lambda i: (i, 0, 0))
     return pl.pallas_call(
         functools.partial(flux_body, slots, group),
-        grid=(slots // group,),
         out_shape=(jax.ShapeDtypeStruct((26 * STEP + 6, 128), F32),)
         + (jax.ShapeDtypeStruct((slots, 32, 128), F32),) * 2,
-        in_specs=[block, block] + [vm()] * 3 + [hbm()],
-        out_specs=(vm(), rim, rim),
+        in_specs=[hbm(), hbm()] + [vm()] * 3 + [hbm()],
+        out_specs=(vm(),) * 3,
         scratch_shapes=[
             pltpu.VMEM((8 * group * MID, 128), jnp.int32),
             pltpu.VMEM((SLOT_ROWS * SLOT_STEP, 128), F32),
             pltpu.VMEM((group * ROW_SIZE, 128), F32),
             pltpu.VMEM((group, LEVELS, TILES, 128), F32),
             pltpu.VMEM((group * MID_SIZE, 128), F32),
+            pltpu.VMEM((2 * group, LEVELS, COLS), F32),
+            pltpu.VMEM((2 * group, LEVELS, COLS), F32),
+            pltpu.SemaphoreType.DMA((2 * group, 2)),
         ],
         compiler_params=pltpu.CompilerParams(vmem_limit_bytes=49 * MIB),
         cost_estimate=pl.CostEstimate(flops=40_000_000, bytes_accessed=15_000_000, transcendentals=0),

time: 71.3 us -> 71.3 us (level)
  waiting for transfers between devices: 8.55 us -> 10.9 us
  Pallas kernels: 33.5 us -> 31.2 us
    pallas_call x3, Pallas kernels: 23.9 us -> 21.5 us  [the longest x2 12.1 us: solve_columns(): pl.pallas_call(functools.partial(solve_body, first, count, extra), out_sh...]
    all_to_all x1, waiting for transfers between devices: 2.79 us -> 4.35 us  [on_device(): got = lax.all_to_all(blocks, 'gx', split_axis=0, concat_axis=0, tiled=True)]
  transfers between devices with their start and end apart: 4 -> 4, of which waited for: 3 -> 3; matrix products, arithmetic and copies ran while one was open for 0% -> 0% of each run, Pallas kernels for 35% -> 32%
where the time goes in v2:
time: 71.3 us; the launch traced here: 70.5 us
  Pallas kernels  31.2 us (44%)
  starting transfers between devices  16.9 us (24%)
  waiting for transfers between devices  10.9 us (15%)
  blocking collectives  6.66 us (9%)
  local copies, waits for them, and re-layouts  4.19 us (6%)
    pallas_call x2, Pallas kernels, solve_columns(): pl.pallas_call(functools.partial(solve_body, first, count, extra), out_sh...  12.1 us
    pallas_call x1, Pallas kernels, face_sums(): pl.pallas_call(functools.partial(flux_body, slots, group), out_shape=(jax...  9.47 us
    all_to_all x1, blocking collectives, across(): return lax.all_to_all(lines, 'gy', split_axis=0, concat_axis=0, tiled=True)  6.66 us
    all_to_all x1, starting transfers between devices, on_device(): edges = lax.all_to_all(table, 'gx', split_axis=0, concat_axis=0, tiled=True)  6.29 us
    all_to_all x1, waiting for transfers between devices, on_device(): got = lax.all_to_all(blocks, 'gx', split_axis=0, concat_axis=0, tiled=True)  4.35 us
    all_to_all x1, starting transfers between devices, across(): return lax.all_to_all(lines, 'gy', split_axis=0, concat_axis=0, tiled=True)  4.24 us
    unnamed x12, local copies, waits for them, and re-layouts  4.19 us
    all_to_all x1, waiting for transfers between devices, on_device(): sums = lax.all_to_all(dots, both, split_axis=0, concat_axis=0, tiled=True)  3.68 us
  transfers between devices with their start and end apart: 4, of which 3 were waited for; matrix products, arithmetic and copies ran while one was open for 0% of the time, Pallas kernels for 32%

profile of v2, /device:TPU:0, one launch (start us, length us, event | category | flops | bytes accessed | tf_op | source)
XLA Modules:
  0.0 70.5 jit_solution(2628362231805412021)
XLA Ops:
  0.6 0.0 copy-start.2
  0.6 0.9 %copy-done.2 = s32[300,180]{0,1:T(8,128)S(1)} copy-done((s32[300,180]{0,1:T(8,128)S(1)}, s32[300,180]{0,1:T(8,128)}, u32[]{:S(2)}) %copy-start.2) | copy-done | bytes 216024
  1.6 0.8 %region_ends.1 = (f32[312,256]{1,0:T(8,128)S(1)}, f32[4,8,256]{2,1,0:T(8,128)}) custom-call(s32[180,300]{1,0:T(8,128)S(1)} %bitcast.10), custom_call_target="tpu_custom_call" | custom-call | tf_op jit(solution)/shard_map/region_ends/pallas_call | solution.py:410
  2.4 4.2 %all-to-all-start = ((f32[4,8,256]{2,1,0:T(8,128)}), f32[4,8,256]{2,1,0:T(8,128)S(1)}, u32[]{:S(2)}, u32[]{:S(2)}) async-start(f32[4,8,256]{2,1,0:T(8,128)} %get-tuple-element.42), calls=%async_computation | async-start | bytes 65536 | tf_op jit(solution)/shard_map/all_to_all | solution.py:1021
  6.6 0.0 copy-start
  6.6 1.0 %copy-done = s32[18,3000]{1,0:T(8,128)S(1)} copy-done((s32[18,3000]{1,0:T(8,128)S(1)}, s32[18,3000]{1,0:T(8,128)}, u32[]{:S(2)}) %copy-start) | copy-done | bytes 216024
  7.6 0.0 copy-start.1
  7.6 1.0 %copy-done.1 = f32[18,3000]{1,0:T(8,128)S(1)} copy-done((f32[18,3000]{1,0:T(8,128)S(1)}, f32[18,3000]{1,0:T(8,128)}, u32[]{:S(2)}) %copy-start.1) | copy-done | bytes 216024
  8.5 0.0 copy-start.3
  8.5 0.7 copy-done.3
  9.2 0.0 copy-start.5
  9.2 0.7 copy-done.5
  9.8 0.9 %column_tables.1 = (s32[608,128]{1,0:T(8,128)S(1)}, f32[608,128]{1,0:T(8,128)S(1)}, f32[720,128]{1,0:T(8,128)S(1)}, f32[96,256]{1,0:T(8,128)S(1)}, f32[24,128]{1...) custom-call(f32[29]{0:T(128)S(1)} %copy-done.5, s32[18]{0:T(128)S(1)} %copy-done.3, s32[18,3000]{1,0:T(8,128)S(1)} %copy-done, ...), custom_call_target="tpu_custom_call" | custom-call | flops 5000000 | bytes 3000000 | tf_op jit(solution)/shard_map/column_tables/pallas_call | solution.py:302
  10.8 0.0 all-to-all-done.lines
  10.8 1.0 %block_edges.1 = (f32[8,32,384]{2,1,0:T(8,128)}, f32[312,256]{1,0:T(8,128)S(1)}, f32[8,128]{1,0:T(8,128)S(1)}) custom-call(f32[312,256]{1,0:T(8,128)S(1)} %get-tuple-element.37.after.depth, f32[4,8,256]{2,1,0:T(8,128)S(1)} %all-to-all-done.lines, f32[8,128]{1,0:T(8,128)S(1)} %get-tuple-element.43.held), custom_call_target="tpu_custom_call" | custom-call | tf_op jit(solution)/shard_map/block_edges/pallas_call | solution.py:383
  11.8 6.3 %all-to-all-start.1 = ((f32[8,32,384]{2,1,0:T(8,128)}), f32[8,32,384]{2,1,0:T(8,128)S(1)}, u32[]{:S(2)}, u32[]{:S(2)}) async-start(f32[8,32,384]{2,1,0:T(8,128)} %get-tuple-element.44), calls=%async_computation.1 | async-start | bytes 786432 | tf_op jit(solution)/shard_map/all_to_all | solution.py:1042
  18.1 0.0 copy-start.4
  18.1 9.5 %face_sums.1 = (f32[656,128]{1,0:T(8,128)S(1)}, f32[18,32,128]{2,1,0:T(8,128)S(1)}, f32[18,32,128]{2,1,0:T(8,128)S(1)}) custom-call(f32[18,30,3000]{2,1,0:T(8,128)} %warm.5, f32[18,30,3000]{2,1,0:T(8,128)} %salt.5, s32[608,128]{1,0:T(8,128)S(1)} %get-tuple-element.38.n_rows, f32[608,128]{1,0:T(8,128)S(1)} %get-tuple-element.39.q_rows, ...), custom_call_target="tpu_custom_call" | custom-call | flops 40000000 | bytes 15000000 | tf_op jit(solution)/shard_map/face_sums/pallas_call | solution.py:578
  27.6 2.8 %all-to-all-done.1 = f32[8,32,384]{2,1,0:T(8,128)S(1)} async-done(((f32[8,32,384]{2,1,0:T(8,128)}), f32[8,32,384]{2,1,0:T(8,128)S(1)}, u32[]{:S(2)}, u32[]{:S(2)}) %all-to-all-start.1) | async-done | bytes 393248 | tf_op jit(solution)/shard_map/all_to_all | solution.py:1042
  30.4 0.0 copy-done.4
  30.4 2.2 %outgoing_blocks.1 = (f32[24,32,128]{2,1,0:T(8,128)}, s32[40,128]{1,0:T(8,128)S(1)}, f32[8,128]{1,0:T(8,128)S(1)}) custom-call(s32[18]{0:T(128)S(1)} %copy-done.4, f32[96,256]{1,0:T(8,128)S(1)} %get-tuple-element.41.pick, f32[256,384]{1,0:T(8,128)S(1)} %bitcast.6, f32[24,128]{1,0:T(8,128)S(1)} %get-tuple-element.45.n_x, ...), custom_call_target="tpu_custom_call" | custom-call | tf_op jit(solution)/shard_map/outgoing_blocks/pallas_call | solution.py:730
  32.6 3.6 %all-to-all-start.2 = ((f32[24,32,128]{2,1,0:T(8,128)}), f32[24,32,128]{2,1,0:T(8,128)S(1)}, u32[]{:S(2)}, u32[]{:S(2)}) async-start(f32[24,32,128]{2,1,0:T(8,128)} %get-tuple-element.55), calls=%async_computation.2 | async-start | bytes 786432 | tf_op jit(solution)/shard_map/all_to_all | solution.py:1046
  36.2 7.5 %column_solve.2 = (f32[18,30,3000]{2,1,0:T(8,128)}, f32[18,30,3000]{2,1,0:T(8,128)}, f32[8,128]{1,0:T(8,128)S(1)}) custom-call(f32[18,30,3000]{2,1,0:T(8,128)} %warm.5, f32[18,30,3000]{2,1,0:T(8,128)} %salt.5, s32[608,128]{1,0:T(8,128)S(1)} %get-tuple-element.38.n_rows, f32[608,128]{1,0:T(8,128)S(1)} %get-tuple-element.39.q_rows, ...), custom_call_target="tpu_custom_call" | custom-call | flops 24000000 | bytes 19200000 | tf_op jit(solution)/shard_map/column_solve/pallas_call | solution.py:212
  43.8 4.4 %all-to-all-done.2 = f32[24,32,128]{2,1,0:T(8,128)S(1)} async-done(((f32[24,32,128]{2,1,0:T(8,128)}), f32[24,32,128]{2,1,0:T(8,128)S(1)}, u32[]{:S(2)}, u32[]{:S(2)}) %all-to-all-start.2) | async-done | bytes 393248 | tf_op jit(solution)/shard_map/all_to_all | solution.py:1046
  48.1 1.4 %region_sums.1 = (f32[624,128]{1,0:T(8,128)S(1)}, f32[4,8,256]{2,1,0:T(8,128)S(1)}, f32[8,256]{1,0:T(8,128)S(1)}) custom-call(s32[40,128]{1,0:T(8,128)S(1)} %get-tuple-element.54.rows, f32[768,128]{1,0:T(8,128)S(1)} %bitcast.8, f32[8,128]{1,0:T(8,128)S(1)} %get-tuple-element.56.after), custom_call_target="tpu_custom_call" | custom-call | tf_op jit(solution)/shard_map/region_sums/pallas_call | solution.py:837
  49.5 6.7 %all_to_all.25.lines = f32[4,8,256]{2,1,0:T(8,128)S(1)} all-to-all(f32[4,8,256]{2,1,0:T(8,128)S(1)} %get-tuple-element.58), channel_id=1, replica_groups=mesh['gx'=8,'gy'=4] {'gy'}, dimensions={0} | all-to-all | bytes 65536 | tf_op jit(solution)/shard_map/all_to_all | solution.py:1021
  56.2 2.2 %krylov_basis.1 = (f32[4,312,256]{2,1,0:T(8,128)S(1)}, f32[312,256]{1,0:T(8,128)S(1)}, f32[32,8,128]{2,1,0:T(8,128)}, f32[8,128]{1,0:T(8,128)S(1)}) custom-call(f32[624,128]{1,0:T(8,128)S(1)} %get-tuple-element.57.region, f32[4,8,256]{2,1,0:T(8,128)S(1)} %all_to_all.25.lines, f32[8,256]{1,0:T(8,128)S(1)} %get-tuple-element.59.folded, ...), custom_call_target="tpu_custom_call" | custom-call | tf_op jit(solution)/shard_map/krylov_basis/pallas_call | solution.py:933
  58.4 2.7 %all-to-all-start.4 = ((f32[32,8,128]{2,1,0:T(8,128)}), f32[32,8,128]{2,1,0:T(8,128)S(1)}, u32[]{:S(2)}, u32[]{:S(2)}) async-start(f32[32,8,128]{2,1,0:T(8,128)} %get-tuple-element.64), calls=%async_computation.4 | async-start | bytes 262144 | tf_op jit(solution)/shard_map/all_to_all | solution.py:1053
  61.1 4.5 %column_solve.3 = (f32[18,30,3000]{2,1,0:T(8,128)}, f32[18,30,3000]{2,1,0:T(8,128)}, f32[8,128]{1,0:T(8,128)S(1)}) custom-call(f32[18,30,3000]{2,1,0:T(8,128)} %warm.5, f32[18,30,3000]{2,1,0:T(8,128)} %salt.5, s32[608,128]{1,0:T(8,128)S(1)} %get-tuple-element.38.n_rows, ...), custom_call_target="tpu_custom_call", output_to_operand_aliasing={{0}: (5, {}), {1}: (6, {})} | custom-call | flops 12000000 | bytes 9600000 | tf_op jit(solution)/shard_map/column_solve/pallas_call | solution.py:212
  65.6 3.7 %all-to-all-done.4 = f32[32,8,128]{2,1,0:T(8,128)S(1)} async-done(((f32[32,8,128]{2,1,0:T(8,128)}), f32[32,8,128]{2,1,0:T(8,128)S(1)}, u32[]{:S(2)}, u32[]{:S(2)}) %all-to-all-start.4) | async-done | bytes 131104 | tf_op jit(solution)/shard_map/all_to_all | solution.py:1053
  69.3 1.2 %combine.1 = (f32[180,300]{1,0:T(8,128)}, f32[180,300]{1,0:T(8,128)}) custom-call(f32[256,128]{1,0:T(8,128)S(1)} %bitcast.9, f32[4,312,256]{2,1,0:T(8,128)S(1)} %get-tuple-element.65.basis, f32[312,256]{1,0:T(8,128)S(1)} %get-tuple-element.66.diagonal, f32[8,128]{1,0:T(8,128)S(1)} %get-tuple-element.67.after), custom_call_target="tpu_custom_call" | custom-call | tf_op jit(solution)/shard_map/combine/pallas_call | solution.py:1010
Async XLA Ops:
  0.6 1.0 %copy-start.2 = (s32[300,180]{0,1:T(8,128)S(1)}, s32[300,180]{0,1:T(8,128)}, u32[]{:S(2)}) copy-start(s32[300,180]{0,1:T(8,128)} %param.13) | copy-start | bytes 648004
  2.4 8.4 %all-to-all-start = ((f32[4,8,256]{2,1,0:T(8,128)}), f32[4,8,256]{2,1,0:T(8,128)S(1)}, u32[]{:S(2)}, u32[]{:S(2)}) async-start(f32[4,8,256]{2,1,0:T(8,128)} %get-tuple-element.42), calls=%async_computation | async-start | bytes 65536 | tf_op jit(solution)/shard_map/all_to_all | solution.py:1021
  6.6 1.0 %copy-start = (s32[18,3000]{1,0:T(8,128)S(1)}, s32[18,3000]{1,0:T(8,128)}, u32[]{:S(2)}) copy-start(s32[18,3000]{1,0:T(8,128)} %depth.1) | copy-start | bytes 648004
  7.6 1.0 %copy-start.1 = (f32[18,3000]{1,0:T(8,128)S(1)}, f32[18,3000]{1,0:T(8,128)}, u32[]{:S(2)}) copy-start(f32[18,3000]{1,0:T(8,128)} %inflow.1) | copy-start | bytes 648004
  8.5 0.7 copy-start.3
  9.2 0.7 copy-start.5
  11.8 18.6 %all-to-all-start.1 = ((f32[8,32,384]{2,1,0:T(8,128)}), f32[8,32,384]{2,1,0:T(8,128)S(1)}, u32[]{:S(2)}, u32[]{:S(2)}) async-start(f32[8,32,384]{2,1,0:T(8,128)} %get-tuple-element.44), calls=%async_computation.1 | async-start | bytes 786432 | tf_op jit(solution)/shard_map/all_to_all | solution.py:1042
  18.1 12.3 %copy-start.4 = (s32[18]{0:T(128)S(1)}, s32[18]{0:T(128)}, u32[]{:S(2)}) copy-start(s32[18]{0:T(128)} %ids.3) | copy-start | bytes 220
  32.6 15.5 %all-to-all-start.2 = ((f32[24,32,128]{2,1,0:T(8,128)}), f32[24,32,128]{2,1,0:T(8,128)S(1)}, u32[]{:S(2)}, u32[]{:S(2)}) async-start(f32[24,32,128]{2,1,0:T(8,128)} %get-tuple-element.55), calls=%async_computation.2 | async-start | bytes 786432 | tf_op jit(solution)/shard_map/all_to_all | solution.py:1046
  58.4 11.0 %all-to-all-start.4 = ((f32[32,8,128]{2,1,0:T(8,128)}), f32[32,8,128]{2,1,0:T(8,128)S(1)}, u32[]{:S(2)}, u32[]{:S(2)}) async-start(f32[32,8,128]{2,1,0:T(8,128)} %get-tuple-element.64), calls=%async_computation.4 | async-start | bytes 262144 | tf_op jit(solution)/shard_map/all_to_all | solution.py:1053

commit v3 on v2

--- a/solution.py
+++ b/solution.py
@@ -226,30 +226,33 @@
     )(warm, salt, *columns, *before, *after)
 
 
-def rim_sources():
-    lane = lax.broadcasted_iota(jnp.int32, (8, 128), 1)
-    one = jnp.where(lane < 64, lane, lane - 64)
-    along_x = jnp.where(one < SPAN_N, one * SPAN_E + jnp.where(lane < 64, 0, SPAN_E - 1), -1)
-    along_y = jnp.where(one < SPAN_E, one + jnp.where(lane < 64, 0, COLS - SPAN_E), -1)
-    return along_x, along_y
-
-
 def lanes_of(x, index):
     return jnp.take_along_axis(x, index, axis=1, mode="promise_in_bounds")
 
 
 def rim_of(tile):
-    sources = rim_sources()
-    used = (range(TILES), (0, TILES - 2, TILES - 1))
-    out = [None, None]
+    lane = lax.broadcasted_iota(jnp.int32, (8, 128), 1)
+    one = lane & 63
+    index = (one * SPAN_E + jnp.where(lane < 64, 0, SPAN_E - 1)) & 127
+    low = high = along = None
     for c in range(TILES):
         now = tile(c)
-        for d in range(2):
-            if c in used[d]:
-                before = out[d] or [jnp.zeros((8, 128), F32)] * len(now)
-                here = (sources[d] >> 7) == c
-                out[d] = [jnp.where(here, lanes_of(v, sources[d] & 127), p) for v, p in zip(now, before)]
-    return out
+        place = lane + 128 * c
+        col = place - SPAN_E * divide(place, SPAN_E)
+        rim = (col == 0) | (col == SPAN_E - 1)
+        if c <= 14:
+            low = now if c == 0 else [jnp.where(rim, v, p) for v, p in zip(now, low)]
+        else:
+            high = now if c == 15 else [jnp.where(rim, v, p) for v, p in zip(now, high)]
+        if c == 0:
+            first = now
+        if c == TILES - 2:
+            along = now
+        if c == TILES - 1:
+            along = [jnp.where(lane >= 124, p, v) for v, p in zip(now, along)]
+    x = [jnp.where(one < 32, lanes_of(p, index), lanes_of(v, index)) for p, v in zip(low, high)]
+    y = [jnp.where(lane < 64, p, pltpu.roll(v, 68, 1)) for p, v in zip(first, along)]
+    return x, y
 
 
 def tables_body(span_x, span_y, mixing, ids, depth, inflow, after, *rest):
@@ -262,8 +265,9 @@
     padded[...] = jnp.zeros((SLOT_ROWS, FLAT), F32)
     padded[0:slots, 0:COLS] = depth[...].astype(F32)
     rims = rim_of(lambda c: [padded[8 * g : 8 * g + 8, c * 128 : c * 128 + 128] for g in range(SLOT_ROWS // 8)])
-    for ref, parts in zip((rim_x, rim_y), rims):
-        ref[...] = jnp.concatenate(parts, axis=0)
+    one = lax.broadcasted_iota(jnp.int32, (1, 128), 1) & 63
+    for ref, parts, used in zip((rim_x, rim_y), rims, (SPAN_N, SPAN_E)):
+        ref[...] = jnp.where(one < used, jnp.concatenate(parts, axis=0), 0.0)
     blocks_x = KX * span_x
     row = lax.broadcasted_iota(jnp.int32, (SLOT_ROWS, 128), 0)
     held = jnp.zeros((SLOT_ROWS, 128), jnp.int32)
@@ -597,7 +601,7 @@
     )(warm, salt, *columns, after)
 
 
-def received_rows(span_x, cap, edges):
+def rows_body(span_x, cap, edges, after, rows):
     blocks_x = KX * span_x
     keys = jnp.concatenate([edges[d * 32 : d * 32 + 1, 256:384] for d in range(span_x)], axis=0).astype(jnp.int32)
     held = jnp.maximum(keys, 0)
@@ -629,11 +633,22 @@
     lines = [jnp.sum(jnp.where(keys == w, at, 0.0), axis=0, keepdims=True) for w in wanted]
     lines += [jnp.zeros((1, 128), F32)] * (ROWS - len(lines))
     sums = jnp.sum(jnp.concatenate(lines, axis=0), axis=1, keepdims=True) - 1.0
-    return jnp.broadcast_to(sums, (ROWS, 128)).astype(jnp.int32)
+    rows[...] = jnp.broadcast_to(sums, (ROWS, 128)).astype(jnp.int32)
+
+
+def received_rows(span_x, cap, edges, after):
+    return pl.pallas_call(
+        functools.partial(rows_body, span_x, cap),
+        out_shape=jax.ShapeDtypeStruct((ROWS, 128), jnp.int32),
+        in_specs=[vm(), hbm()],
+        out_specs=vm(),
+        compiler_params=pltpu.CompilerParams(vmem_limit_bytes=12 * MIB),
+        name="received_rows",
+    )(edges, after)
 
 
 def outgoing_body(
-    span_x, cap, slots, ids, pick, edges, n_x, n_y, inside, rim_x, rim_y, out, rows, _, pieces, q_x, q_y, source, counts
+    span_x, cap, slots, ids, pick, edges, n_x, n_y, inside, rim_x, rim_y, out, _, pieces, q_x, q_y, source, counts
 ):
     blocks_x = KX * span_x
     for d in range(span_x):
@@ -650,7 +665,6 @@
             source[owner * cap + jnp.minimum(rank, cap - 1)] = s
             counts[owner] = rank + 1
 
-    rows[...] = received_rows(span_x, cap, edges)
     near = jnp.dot(
         pick[...].astype(jnp.bfloat16), edges[:, 0:GX].astype(jnp.bfloat16), preferred_element_type=F32
     )
@@ -729,13 +743,9 @@
     slots = ids.shape[0]
     return pl.pallas_call(
         functools.partial(outgoing_body, span_x, cap, slots),
-        out_shape=(
-            jax.ShapeDtypeStruct((span_x * cap, 32, 128), F32),
-            jax.ShapeDtypeStruct((ROWS, 128), jnp.int32),
-            mark_shape(),
-        ),
+        out_shape=(jax.ShapeDtypeStruct((span_x * cap, 32, 128), F32), mark_shape()),
         in_specs=[sm()] + [vm()] * 7,
-        out_specs=(vm(), vm(), hbm()),
+        out_specs=(vm(), hbm()),
         scratch_shapes=[pltpu.VMEM((32 * STEP + 8, 128), F32)]
         + [pltpu.VMEM((SLOT_ROWS, 128), F32)] * 2
         + [pltpu.SMEM((span_x * cap,), jnp.int32), pltpu.SMEM((span_x,), jnp.int32)],
@@ -849,7 +859,23 @@
     )(rows, got.reshape(-1, 128), after)
 
 
-def basis_body(span_x, span_y, region, lines, folded, extended, edges, basis, diag_out, dots, mark):
+def south_of(x):
+    return pltpu.roll(x, 1, 0)
+
+
+def north_of(x):
+    return pltpu.roll(x, GY - 1, 0)
+
+
+def west_of(x):
+    return pltpu.roll(x, 1, 1)
+
+
+def east_of(x):
+    return pltpu.roll(x, GX - 1, 1)
+
+
+def weights_body(span_x, span_y, extended, edges, after, *out):
     ext = extended[...]
     here = lax.axis_index("gx")
     lane8 = lax.broadcasted_iota(jnp.int32, (8, GX), 1)
@@ -874,24 +900,30 @@
     beyond = jnp.where(lax.axis_index("gy") == span_y - 1, beyond, 0.0)
     ext = ext + jnp.concatenate([jnp.zeros((RY, GX), F32), beyond, jnp.zeros((GY - RY - 4, GX), F32)], axis=0)
 
-    def south_of(x):
-        return pltpu.roll(x, 1, 0)
-
-    def north_of(x):
-        return pltpu.roll(x, GY - 1, 0)
-
-    def west_of(x):
-        return pltpu.roll(x, 1, 1)
-
-    def east_of(x):
-        return pltpu.roll(x, GX - 1, 1)
-
     to_east = jnp.minimum(ext, east_of(ext)) / LEVELS
     to_north = jnp.minimum(ext, north_of(ext)) / LEVELS
     to_west = west_of(to_east)
     to_south = south_of(to_north)
     diagonal = jnp.where(ext > 0, DAMPING, 1.0) + to_east + to_west + to_north + to_south
     inverse = 1.0 / diagonal
+    for ref, value in zip(out, (to_east, to_west, to_north, to_south, diagonal, inverse)):
+        ref[...] = value
+
+
+def face_weights(span_x, span_y, extended, edges, after):
+    return pl.pallas_call(
+        functools.partial(weights_body, span_x, span_y),
+        out_shape=(jax.ShapeDtypeStruct((GY, GX), F32),) * 6,
+        in_specs=[vm()] * 2 + [hbm()],
+        out_specs=(vm(),) * 6,
+        compiler_params=pltpu.CompilerParams(vmem_limit_bytes=12 * MIB),
+        name="face_weights",
+    )(extended, edges, after)
+
+
+def basis_body(span_y, region, lines, folded, east, west, north, south, diag_in, inv_in, basis, dots, mark):
+    to_east, to_west, to_north, to_south = east[...], west[...], north[...], south[...]
+    diagonal, inverse = diag_in[...], inv_in[...]
     ups, downs = beside_lines(span_y, lines, folded[...])
     partial = jnp.concatenate([region[0:GY, :], region[GY : 2 * GY, :]], axis=1)
     gap = lambda rows: jnp.zeros((rows, GX), F32)
@@ -911,7 +943,6 @@
     lane = lax.broadcasted_iota(jnp.int32, (GY, GX), 1)
     row = lax.broadcasted_iota(jnp.int32, (GY, GX), 0)
     inside = (lane < RX) & (row < RY)
-    diag_out[...] = diagonal
     clean = [jnp.where(inside, v, 0.0) for v in vectors]
     position = lax.broadcasted_iota(jnp.int32, (8, 128), 1)
     packed = jnp.zeros((8, 128), F32)
@@ -929,20 +960,19 @@
         dots[d] = packed
 
 
-def krylov_basis(span_x, span_y, region, lines, folded, extended, edges):
+def krylov_basis(span_x, span_y, region, lines, folded, weights):
     return pl.pallas_call(
-        functools.partial(basis_body, span_x, span_y),
+        functools.partial(basis_body, span_y),
         out_shape=(
             jax.ShapeDtypeStruct((4, GY, GX), F32),
-            jax.ShapeDtypeStruct((GY, GX), F32),
             jax.ShapeDtypeStruct((span_x * span_y, 8, 128), F32),
             mark_shape(),
         ),
-        in_specs=[vm()] * 5,
-        out_specs=(vm(),) * 3 + (hbm(),),
+        in_specs=[vm()] * 9,
+        out_specs=(vm(),) * 2 + (hbm(),),
         compiler_params=pltpu.CompilerParams(vmem_limit_bytes=12 * MIB),
         name="krylov_basis",
-    )(region, lines, folded, extended, edges)
+    )(region, lines, folded, *weights)
 
 
 def combine_body(dots, basis, diagonal, after, height, misfit):
@@ -1027,7 +1057,7 @@
     slots = tiles.shape[0]
     cap = (KX * KY + span_x - 1) // span_x
     both = ("gx", "gy")
-    bounds = [slots * i // 18 for i in (0, 12, 18)]
+    bounds = [slots * i // 18 for i in (0, 13, 18)]
 
     def solve(part, before, after):
         first, end = bounds[part], bounds[part + 1]
@@ -1042,17 +1072,17 @@
     edges = lax.all_to_all(table, "gx", split_axis=0, concat_axis=0, tiled=True)
     sums = face_sums(warm, salt, columns, mark)
     flat_edges = edges.reshape(-1, EDGE)
-    blocks, rows, mark = outgoing_blocks(span_x, cap, tiles, pick, flat_edges, (n_x, n_y), sums)
+    blocks, mark = outgoing_blocks(span_x, cap, tiles, pick, flat_edges, (n_x, n_y), sums)
+    rows = received_rows(span_x, cap, flat_edges, mark)
     got = lax.all_to_all(blocks, "gx", split_axis=0, concat_axis=0, tiled=True)
     *solved, done = solve(0, (), mark)
 
     region, lines, folded = region_sums(span_y, rows, got, done)
-    basis, diagonal, dots, mark = krylov_basis(
-        span_x, span_y, region, across(lines), folded, extended, flat_edges
-    )
+    weights = face_weights(span_x, span_y, extended, flat_edges, region)
+    basis, dots, mark = krylov_basis(span_x, span_y, region, across(lines), folded, weights)
     sums = lax.all_to_all(dots, both, split_axis=0, concat_axis=0, tiled=True)
     *solved, done = solve(1, solved, mark)
-    height, misfit = combine(sums.reshape(-1, 128), basis, diagonal, done)
+    height, misfit = combine(sums.reshape(-1, 128), basis, weights[4], done)
     return (solved[0], solved[1], height.T, misfit.T)
 
 

time: 71.3 us -> 78.7 us (1.10)
  local copies, waits for them, and re-layouts: 4.19 us -> 12.7 us
  blocking collectives: 6.66 us -> 0 us
  starting transfers between devices: 16.9 us -> 21.6 us
    unnamed x12 -> x32, local copies, waits for them, and re-layouts: 4.19 us -> 12.7 us
    all_to_all x1 -> x0, blocking collectives: 6.66 us -> none  [across(): return lax.all_to_all(lines, 'gy', split_axis=0, concat_axis=0, tiled=True)]
    all_to_all x1 -> x2, starting transfers between devices: 4.24 us -> 7.5 us  [across(): return lax.all_to_all(lines, 'gy', split_axis=0, concat_axis=0, tiled=True)]
    all_to_all x1, starting transfers between devices: 2.72 us -> 4.14 us  [on_device(): sums = lax.all_to_all(dots, both, split_axis=0, concat_axis=0, tiled=True)]
    all_to_all x1, waiting for transfers between devices: 4.35 us -> 3.34 us  [on_device(): got = lax.all_to_all(blocks, 'gx', split_axis=0, concat_axis=0, tiled=True)]
    all_to_all x1, waiting for transfers between devices: 3.68 us -> 4.53 us  [on_device(): sums = lax.all_to_all(dots, both, split_axis=0, concat_axis=0, tiled=True)]
    pallas_call x1 -> x3, Pallas kernels: 2.18 us -> 2.58 us  [the longest x1 1.85 us: krylov_basis(): pl.pallas_call(functools.partial(basis_body, span_y), out_shape=(jax.Shap...]
  transfers between devices with their start and end apart: 4 -> 5, of which waited for: 3 -> 3; matrix products, arithmetic and copies ran while one was open for 0% -> 0% of each run, Pallas kernels for 32% -> 29%
where the time goes in v3:
time: 78.7 us; the launch traced here: 77.6 us
  Pallas kernels  31.5 us (40%)
  starting transfers between devices  21.6 us (27%)
  local copies, waits for them, and re-layouts  12.7 us (16%)
  waiting for transfers between devices  11.1 us (14%)
    unnamed x32, local copies, waits for them, and re-layouts  12.7 us
    pallas_call x2, Pallas kernels, solve_columns(): pl.pallas_call(functools.partial(solve_body, first, count, extra), out_sh...  12 us
    pallas_call x1, Pallas kernels, face_sums(): pl.pallas_call(functools.partial(flux_body, slots, group), out_shape=(jax...  9.05 us
    all_to_all x2, starting transfers between devices, across(): return lax.all_to_all(lines, 'gy', split_axis=0, concat_axis=0, tiled=True)  7.5 us
    all_to_all x1, starting transfers between devices, on_device(): edges = lax.all_to_all(table, 'gx', split_axis=0, concat_axis=0, tiled=True)  6.29 us
    all_to_all x1, waiting for transfers between devices, on_device(): sums = lax.all_to_all(dots, both, split_axis=0, concat_axis=0, tiled=True)  4.53 us
    all_to_all x1, starting transfers between devices, on_device(): sums = lax.all_to_all(dots, both, split_axis=0, concat_axis=0, tiled=True)  4.14 us
    all_to_all x1, starting transfers between devices, on_device(): got = lax.all_to_all(blocks, 'gx', split_axis=0, concat_axis=0, tiled=True)  3.63 us
  transfers between devices with their start and end apart: 5, of which 3 were waited for; matrix products, arithmetic and copies ran while one was open for 0% of the time, Pallas kernels for 29%

profile of v3, /device:TPU:0, one launch (start us, length us, event | category | flops | bytes accessed | tf_op | source)
XLA Modules:
  0.0 77.6 jit_solution(7058732365894564500)
XLA Ops:
  0.6 0.9 %copy-done.12 = s32[300,180]{0,1:T(8,128)S(1)} copy-done((s32[300,180]{0,1:T(8,128)S(1)}, s32[300,180]{0,1:T(8,128)}, u32[]{:S(2)}) %copy-start.12) | copy-done | bytes 216024
  1.6 0.8 %region_ends.1 = (f32[312,256]{1,0:T(8,128)S(1)}, f32[4,8,256]{2,1,0:T(8,128)}) custom-call(s32[180,300]{1,0:T(8,128)S(1)} %bitcast.11), custom_call_target="tpu_custom_call" | custom-call | tf_op jit(solution)/shard_map/region_ends/pallas_call | solution.py:414
  2.4 4.2 %all-to-all-start = ((f32[4,8,256]{2,1,0:T(8,128)}), f32[4,8,256]{2,1,0:T(8,128)S(1)}, u32[]{:S(2)}, u32[]{:S(2)}) async-start(f32[4,8,256]{2,1,0:T(8,128)} %get-tuple-element.46), calls=%async_computation | async-start | bytes 65536 | tf_op jit(solution)/shard_map/all_to_all | solution.py:1051
  6.6 1.0 %copy-done.10 = s32[18,3000]{1,0:T(8,128)S(1)} copy-done((s32[18,3000]{1,0:T(8,128)S(1)}, s32[18,3000]{1,0:T(8,128)}, u32[]{:S(2)}) %copy-start.10) | copy-done | bytes 216024
  7.6 1.0 %copy-done.11 = f32[18,3000]{1,0:T(8,128)S(1)} copy-done((f32[18,3000]{1,0:T(8,128)S(1)}, f32[18,3000]{1,0:T(8,128)}, u32[]{:S(2)}) %copy-start.11) | copy-done | bytes 216024
  8.5 0.7 copy-done.13
  9.8 0.9 %column_tables.1 = (s32[608,128]{1,0:T(8,128)S(1)}, f32[608,128]{1,0:T(8,128)S(1)}, f32[720,128]{1,0:T(8,128)S(1)}, f32[96,256]{1,0:T(8,128)S(1)}, f32[24,128]{1...) custom-call(f32[29]{0:T(128)S(1)} %copy-done.15, s32[18]{0:T(128)S(1)} %copy-done.13, ...), custom_call_target="tpu_custom_call" | custom-call | flops 5000000 | bytes 3000000 | tf_op jit(solution)/shard_map/column_tables/pallas_call | solution.py:306
  10.7 1.0 %block_edges.1 = (f32[8,32,384]{2,1,0:T(8,128)}, f32[312,256]{1,0:T(8,128)S(1)}, f32[8,128]{1,0:T(8,128)S(1)}) custom-call(f32[312,256]{1,0:T(8,128)S(1)} %get-tuple-element.41.after.depth, f32[4,8,256]{2,1,0:T(8,128)S(1)} %all-to-all-done.lines, f32[8,128]{1,0:T(8,128)S(1)} %get-tuple-element.47.held), custom_call_target="tpu_custom_call" | custom-call | tf_op jit(solution)/shard_map/block_edges/pallas_call | solution.py:387
  11.8 6.3 %all-to-all-start.1 = ((f32[8,32,384]{2,1,0:T(8,128)}), f32[8,32,384]{2,1,0:T(8,128)S(1)}, u32[]{:S(2)}, u32[]{:S(2)}) async-start(f32[8,32,384]{2,1,0:T(8,128)} %get-tuple-element.48), calls=%async_computation.1 | async-start | bytes 786432 | tf_op jit(solution)/shard_map/all_to_all | solution.py:1072
  18.1 9.1 %face_sums.1 = (f32[656,128]{1,0:T(8,128)S(1)}, f32[18,32,128]{2,1,0:T(8,128)S(1)}, f32[18,32,128]{2,1,0:T(8,128)S(1)}) custom-call(f32[18,30,3000]{2,1,0:T(8,128)} %warm.5, f32[18,30,3000]{2,1,0:T(8,128)} %salt.5, s32[608,128]{1,0:T(8,128)S(1)} %get-tuple-element.42.n_rows, f32[608,128]{1,0:T(8,128)S(1)} %get-tuple-element.43.q_rows, ...), custom_call_target="tpu_custom_call" | custom-call | flops 40000000 | bytes 15000000 | tf_op jit(solution)/shard_map/face_sums/pallas_call | solution.py:582
  27.1 3.2 %all-to-all-done.1 = f32[8,32,384]{2,1,0:T(8,128)S(1)} async-done(((f32[8,32,384]{2,1,0:T(8,128)}), f32[8,32,384]{2,1,0:T(8,128)S(1)}, u32[]{:S(2)}, u32[]{:S(2)}) %all-to-all-start.1) | async-done | bytes 393248 | tf_op jit(solution)/shard_map/all_to_all | solution.py:1072
  30.4 2.1 %outgoing_blocks.1 = (f32[24,32,128]{2,1,0:T(8,128)}, f32[8,128]{1,0:T(8,128)S(1)}) custom-call(s32[18]{0:T(128)S(1)} %copy-done.14, f32[96,256]{1,0:T(8,128)S(1)} %get-tuple-element.45.pick, f32[256,384]{1,0:T(8,128)S(1)} %bitcast.6, f32[24,128]{1,0:T(8,128)S(1)} %get-tuple-element.49.n_x, f32[24,128]{1,0:T(8,128)S(1)} %get-tuple-element.50.n_y, ...), custom_call_target="tpu_custom_call" | custom-call | tf_op jit(solution)/shard_map/outgoing_blocks/pallas_call | solution.py:744
  32.5 3.6 %all-to-all-start.2 = ((f32[24,32,128]{2,1,0:T(8,128)}), f32[24,32,128]{2,1,0:T(8,128)S(1)}, u32[]{:S(2)}, u32[]{:S(2)}) async-start(f32[24,32,128]{2,1,0:T(8,128)} %get-tuple-element.58), calls=%async_computation.2 | async-start | bytes 786432 | tf_op jit(solution)/shard_map/all_to_all | solution.py:1077
  36.4 8.3 %column_solve.2 = (f32[18,30,3000]{2,1,0:T(8,128)}, f32[18,30,3000]{2,1,0:T(8,128)}, f32[8,128]{1,0:T(8,128)S(1)}) custom-call(f32[18,30,3000]{2,1,0:T(8,128)} %warm.5, f32[18,30,3000]{2,1,0:T(8,128)} %salt.5, s32[608,128]{1,0:T(8,128)S(1)} %get-tuple-element.42.n_rows, f32[608,128]{1,0:T(8,128)S(1)} %get-tuple-element.43.q_rows, ...), custom_call_target="tpu_custom_call" | custom-call | flops 26000000 | bytes 20800000 | tf_op jit(solution)/shard_map/column_solve/pallas_call | solution.py:212
  44.7 3.3 %all-to-all-done.2 = f32[24,32,128]{2,1,0:T(8,128)S(1)} async-done(((f32[24,32,128]{2,1,0:T(8,128)}), f32[24,32,128]{2,1,0:T(8,128)S(1)}, u32[]{:S(2)}, u32[]{:S(2)}) %all-to-all-start.2) | async-done | bytes 393248 | tf_op jit(solution)/shard_map/all_to_all | solution.py:1077
  48.1 1.9 %region_sums.1 = (f32[624,128]{1,0:T(8,128)S(1)}, f32[4,8,256]{2,1,0:T(8,128)}, f32[8,256]{1,0:T(8,128)S(1)}) custom-call(s32[40,128]{1,0:T(8,128)S(1)} %received_rows.1.rows, f32[768,128]{1,0:T(8,128)S(1)} %bitcast.9, f32[8,128]{1,0:T(8,128)S(1)} %get-tuple-element.59.after), custom_call_target="tpu_custom_call" | custom-call | tf_op jit(solution)/shard_map/region_sums/pallas_call | solution.py:847
  50.0 3.3 %all-to-all-start.3 = ((f32[4,8,256]{2,1,0:T(8,128)}), f32[4,8,256]{2,1,0:T(8,128)S(1)}, u32[]{:S(2)}, u32[]{:S(2)}) async-start(f32[4,8,256]{2,1,0:T(8,128)} %get-tuple-element.61), calls=%async_computation.3 | async-start | bytes 65536 | tf_op jit(solution)/shard_map/all_to_all | solution.py:1051
  53.7 0.7 copy-done
  54.4 0.7 copy-done.2
  55.2 0.7 copy-done.4
  55.9 0.7 copy-done.6
  56.6 0.7 copy-done.8
  57.4 1.0 %copy-done.1 = f32[312,256]{1,0:T(8,128)S(1)} copy-done((f32[312,256]{1,0:T(8,128)S(1)}, f32[312,256]{1,0:T(8,128)}, u32[]{:S(2)}) %copy-start.1) | copy-done | bytes 319512
  58.3 1.0 %copy-done.3 = f32[312,256]{1,0:T(8,128)S(1)} copy-done((f32[312,256]{1,0:T(8,128)S(1)}, f32[312,256]{1,0:T(8,128)}, u32[]{:S(2)}) %copy-start.3) | copy-done | bytes 319512
  59.3 1.0 %copy-done.5 = f32[312,256]{1,0:T(8,128)S(1)} copy-done((f32[312,256]{1,0:T(8,128)S(1)}, f32[312,256]{1,0:T(8,128)}, u32[]{:S(2)}) %copy-start.5) | copy-done | bytes 319512
  60.3 1.0 %copy-done.7 = f32[312,256]{1,0:T(8,128)S(1)} copy-done((f32[312,256]{1,0:T(8,128)S(1)}, f32[312,256]{1,0:T(8,128)}, u32[]{:S(2)}) %copy-start.7) | copy-done | bytes 319512
  61.3 1.0 %copy-done.9 = f32[312,256]{1,0:T(8,128)S(1)} copy-done((f32[312,256]{1,0:T(8,128)S(1)}, f32[312,256]{1,0:T(8,128)}, u32[]{:S(2)}) %copy-start.9) | copy-done | bytes 319512
  62.2 1.9 %krylov_basis.1 = (f32[4,312,256]{2,1,0:T(8,128)S(1)}, f32[32,8,128]{2,1,0:T(8,128)}, f32[8,128]{1,0:T(8,128)S(1)}) custom-call(f32[624,128]{1,0:T(8,128)S(1)} %get-tuple-element.60.after.region, f32[4,8,256]{2,1,0:T(8,128)S(1)} %all-to-all-done.3.lines, f32[8,256]{1,0:T(8,128)S(1)} %get-tuple-element.62.folded, f32[312,256]{1,0:T(8,128)S(1)} %copy-done.1, ...), custom_call_target="tpu_custom_call" | custom-call | tf_op jit(solution)/shard_map/krylov_basis/pallas_call | solution.py:964
  64.1 4.1 %all-to-all-start.4 = ((f32[32,8,128]{2,1,0:T(8,128)}), f32[32,8,128]{2,1,0:T(8,128)S(1)}, u32[]{:S(2)}, u32[]{:S(2)}) async-start(f32[32,8,128]{2,1,0:T(8,128)} %get-tuple-element.73), calls=%async_computation.4 | async-start | bytes 262144 | tf_op jit(solution)/shard_map/all_to_all | solution.py:1083
  68.2 3.7 %column_solve.3 = (f32[18,30,3000]{2,1,0:T(8,128)}, f32[18,30,3000]{2,1,0:T(8,128)}, f32[8,128]{1,0:T(8,128)S(1)}) custom-call(f32[18,30,3000]{2,1,0:T(8,128)} %warm.5, f32[18,30,3000]{2,1,0:T(8,128)} %salt.5, s32[608,128]{1,0:T(8,128)S(1)} %get-tuple-element.42.n_rows, ...), custom_call_target="tpu_custom_call", output_to_operand_aliasing={{0}: (5, {}), {1}: (6, {})} | custom-call | flops 10000000 | bytes 8000000 | tf_op jit(solution)/shard_map/column_solve/pallas_call | solution.py:212
  71.9 4.5 %all-to-all-done.4 = f32[32,8,128]{2,1,0:T(8,128)S(1)} async-done(((f32[32,8,128]{2,1,0:T(8,128)}), f32[32,8,128]{2,1,0:T(8,128)S(1)}, u32[]{:S(2)}, u32[]{:S(2)}) %all-to-all-start.4) | async-done | bytes 131104 | tf_op jit(solution)/shard_map/all_to_all | solution.py:1083
  76.5 1.2 %combine.1 = (f32[180,300]{1,0:T(8,128)}, f32[180,300]{1,0:T(8,128)}) custom-call(f32[256,128]{1,0:T(8,128)S(1)} %bitcast.10, f32[4,312,256]{2,1,0:T(8,128)S(1)} %get-tuple-element.74.basis, f32[312,256]{1,0:T(8,128)S(1)} %get-tuple-element.68.diag_in.diagonal, f32[8,128]{1,0:T(8,128)S(1)} %get-tuple-element.75.after), custom_call_target="tpu_custom_call" | custom-call | tf_op jit(solution)/shard_map/combine/pallas_call | solution.py:1040
  (22 shorter events, 1.4 us)
Async XLA Ops:
  0.6 1.0 %copy-start.12 = (s32[300,180]{0,1:T(8,128)S(1)}, s32[300,180]{0,1:T(8,128)}, u32[]{:S(2)}) copy-start(s32[300,180]{0,1:T(8,128)} %param.13) | copy-start | bytes 648004
  2.4 8.4 %all-to-all-start = ((f32[4,8,256]{2,1,0:T(8,128)}), f32[4,8,256]{2,1,0:T(8,128)S(1)}, u32[]{:S(2)}, u32[]{:S(2)}) async-start(f32[4,8,256]{2,1,0:T(8,128)} %get-tuple-element.46), calls=%async_computation | async-start | bytes 65536 | tf_op jit(solution)/shard_map/all_to_all | solution.py:1051
  6.6 1.0 %copy-start.10 = (s32[18,3000]{1,0:T(8,128)S(1)}, s32[18,3000]{1,0:T(8,128)}, u32[]{:S(2)}) copy-start(s32[18,3000]{1,0:T(8,128)} %depth.1) | copy-start | bytes 648004
  7.6 1.0 %copy-start.11 = (f32[18,3000]{1,0:T(8,128)S(1)}, f32[18,3000]{1,0:T(8,128)}, u32[]{:S(2)}) copy-start(f32[18,3000]{1,0:T(8,128)} %inflow.1) | copy-start | bytes 648004
  8.5 0.7 copy-start.13
  9.2 0.7 copy-start.15
  11.8 18.6 %all-to-all-start.1 = ((f32[8,32,384]{2,1,0:T(8,128)}), f32[8,32,384]{2,1,0:T(8,128)S(1)}, u32[]{:S(2)}, u32[]{:S(2)}) async-start(f32[8,32,384]{2,1,0:T(8,128)} %get-tuple-element.48), calls=%async_computation.1 | async-start | bytes 786432 | tf_op jit(solution)/shard_map/all_to_all | solution.py:1072
  18.1 12.3 %copy-start.14 = (s32[18]{0:T(128)S(1)}, s32[18]{0:T(128)}, u32[]{:S(2)}) copy-start(s32[18]{0:T(128)} %ids.3) | copy-start | bytes 220
  32.5 15.5 %all-to-all-start.2 = ((f32[24,32,128]{2,1,0:T(8,128)}), f32[24,32,128]{2,1,0:T(8,128)S(1)}, u32[]{:S(2)}, u32[]{:S(2)}) async-start(f32[24,32,128]{2,1,0:T(8,128)} %get-tuple-element.58), calls=%async_computation.2 | async-start | bytes 786432 | tf_op jit(solution)/shard_map/all_to_all | solution.py:1077
  50.0 7.4 %all-to-all-start.3 = ((f32[4,8,256]{2,1,0:T(8,128)}), f32[4,8,256]{2,1,0:T(8,128)S(1)}, u32[]{:S(2)}, u32[]{:S(2)}) async-start(f32[4,8,256]{2,1,0:T(8,128)} %get-tuple-element.61), calls=%async_computation.3 | async-start | bytes 65536 | tf_op jit(solution)/shard_map/all_to_all | solution.py:1051
  53.7 0.7 copy-start
  54.4 0.7 copy-start.2
  55.2 0.7 copy-start.4
  55.9 0.7 copy-start.6
  56.6 0.7 copy-start.8
  57.4 1.0 %copy-start.1 = (f32[312,256]{1,0:T(8,128)S(1)}, f32[312,256]{1,0:T(8,128)}, u32[]{:S(2)}) copy-start(f32[312,256]{1,0:T(8,128)} %copy-done) | copy-start | bytes 958468
  58.3 1.0 %copy-start.3 = (f32[312,256]{1,0:T(8,128)S(1)}, f32[312,256]{1,0:T(8,128)}, u32[]{:S(2)}) copy-start(f32[312,256]{1,0:T(8,128)} %copy-done.2) | copy-start | bytes 958468
  59.3 1.0 %copy-start.5 = (f32[312,256]{1,0:T(8,128)S(1)}, f32[312,256]{1,0:T(8,128)}, u32[]{:S(2)}) copy-start(f32[312,256]{1,0:T(8,128)} %copy-done.4) | copy-start | bytes 958468
  60.3 1.0 %copy-start.7 = (f32[312,256]{1,0:T(8,128)S(1)}, f32[312,256]{1,0:T(8,128)}, u32[]{:S(2)}) copy-start(f32[312,256]{1,0:T(8,128)} %copy-done.6) | copy-start | bytes 958468
  61.3 1.0 %copy-start.9 = (f32[312,256]{1,0:T(8,128)S(1)}, f32[312,256]{1,0:T(8,128)}, u32[]{:S(2)}) copy-start(f32[312,256]{1,0:T(8,128)} %copy-done.8) | copy-start | bytes 958468
  64.1 12.4 %all-to-all-start.4 = ((f32[32,8,128]{2,1,0:T(8,128)}), f32[32,8,128]{2,1,0:T(8,128)S(1)}, u32[]{:S(2)}, u32[]{:S(2)}) async-start(f32[32,8,128]{2,1,0:T(8,128)} %get-tuple-element.73), calls=%async_computation.4 | async-start | bytes 262144 | tf_op jit(solution)/shard_map/all_to_all | solution.py:1083

commit v4 on v2

--- a/solution.py
+++ b/solution.py
@@ -226,30 +226,33 @@
     )(warm, salt, *columns, *before, *after)
 
 
-def rim_sources():
-    lane = lax.broadcasted_iota(jnp.int32, (8, 128), 1)
-    one = jnp.where(lane < 64, lane, lane - 64)
-    along_x = jnp.where(one < SPAN_N, one * SPAN_E + jnp.where(lane < 64, 0, SPAN_E - 1), -1)
-    along_y = jnp.where(one < SPAN_E, one + jnp.where(lane < 64, 0, COLS - SPAN_E), -1)
-    return along_x, along_y
-
-
 def lanes_of(x, index):
     return jnp.take_along_axis(x, index, axis=1, mode="promise_in_bounds")
 
 
 def rim_of(tile):
-    sources = rim_sources()
-    used = (range(TILES), (0, TILES - 2, TILES - 1))
-    out = [None, None]
+    lane = lax.broadcasted_iota(jnp.int32, (8, 128), 1)
+    one = lane & 63
+    index = (one * SPAN_E + jnp.where(lane < 64, 0, SPAN_E - 1)) & 127
+    low = high = along = None
     for c in range(TILES):
         now = tile(c)
-        for d in range(2):
-            if c in used[d]:
-                before = out[d] or [jnp.zeros((8, 128), F32)] * len(now)
-                here = (sources[d] >> 7) == c
-                out[d] = [jnp.where(here, lanes_of(v, sources[d] & 127), p) for v, p in zip(now, before)]
-    return out
+        place = lane + 128 * c
+        col = place - SPAN_E * divide(place, SPAN_E)
+        rim = (col == 0) | (col == SPAN_E - 1)
+        if c <= 14:
+            low = now if c == 0 else [jnp.where(rim, v, p) for v, p in zip(now, low)]
+        else:
+            high = now if c == 15 else [jnp.where(rim, v, p) for v, p in zip(now, high)]
+        if c == 0:
+            first = now
+        if c == TILES - 2:
+            along = now
+        if c == TILES - 1:
+            along = [jnp.where(lane >= 124, p, v) for v, p in zip(now, along)]
+    x = [jnp.where(one < 32, lanes_of(p, index), lanes_of(v, index)) for p, v in zip(low, high)]
+    y = [jnp.where(lane < 64, p, pltpu.roll(v, 68, 1)) for p, v in zip(first, along)]
+    return x, y
 
 
 def tables_body(span_x, span_y, mixing, ids, depth, inflow, after, *rest):
@@ -262,8 +265,9 @@
     padded[...] = jnp.zeros((SLOT_ROWS, FLAT), F32)
     padded[0:slots, 0:COLS] = depth[...].astype(F32)
     rims = rim_of(lambda c: [padded[8 * g : 8 * g + 8, c * 128 : c * 128 + 128] for g in range(SLOT_ROWS // 8)])
-    for ref, parts in zip((rim_x, rim_y), rims):
-        ref[...] = jnp.concatenate(parts, axis=0)
+    one = lax.broadcasted_iota(jnp.int32, (1, 128), 1) & 63
+    for ref, parts, used in zip((rim_x, rim_y), rims, (SPAN_N, SPAN_E)):
+        ref[...] = jnp.where(one < used, jnp.concatenate(parts, axis=0), 0.0)
     blocks_x = KX * span_x
     row = lax.broadcasted_iota(jnp.int32, (SLOT_ROWS, 128), 0)
     held = jnp.zeros((SLOT_ROWS, 128), jnp.int32)
@@ -331,7 +335,7 @@
     return ups, downs
 
 
-def edges_body(span_x, span_y, depth, lines, held, table, extended, _, rows):
+def edges_body(span_x, span_y, depth, lines, held, out, extended, _, rows, table, sent):
     ups, downs = beside_lines(span_y, lines, 0.0)
     top = lax.axis_index("gy") == span_y - 1
     extended[...] = depth[...]
@@ -361,22 +365,25 @@
         a = pltpu.roll(low, (192 - b * SPAN_E) % GX, 1)
         z = pltpu.roll(high, (128 - b * SPAN_E) % GX, 1)
         both = jnp.where(lane >= 192, a, z)
-        table[0, 8 * b : 8 * b + 8, 128:256] = both[:, 128:256]
-        table[0, 8 * b : 8 * b + 8, 0:128] = jnp.zeros((8, 128), F32)
-        table[0, 8 * b : 8 * b + 8, 256:384] = jnp.zeros((8, 128), F32)
+        table[8 * b : 8 * b + 8, 128:256] = both[:, 128:256]
+        table[8 * b : 8 * b + 8, 0:128] = jnp.zeros((8, 128), F32)
+        table[8 * b : 8 * b + 8, 256:384] = jnp.zeros((8, 128), F32)
     for m in range(KY):
         z = pltpu.roll(sides, (EDGE - m * SPAN_N) % EDGE, 1)[:, 0:128]
         a = pltpu.roll(sides, (EDGE + 64 - m * SPAN_N) % EDGE, 1)[:, 0:128]
         for b in range(KX):
-            table[0, 8 * b + m + 1 : 8 * b + m + 2, 0:128] = jnp.where(
+            table[8 * b + m + 1 : 8 * b + m + 2, 0:128] = jnp.where(
                 lane1[0:1] >= 64, a[b : b + 1], z[3 + b : 4 + b]
             )
-    table[0, 0:1, 256:384] = held[0:1, :]
-    table[0, 8:12, 256:384] = turned[0:4, 0:128]
-    table[0, 12:16, 256:384] = turned[0:4, 128:256]
-    table[0, 24:32, :] = columns(jnp.where(pick < 4, pick, RX - 8 + pick))
-    for d in range(1, span_x):
-        table[d] = table[0]
+    table[0:1, 256:384] = held[0:1, :]
+    table[8:12, 256:384] = turned[0:4, 0:128]
+    table[12:16, 256:384] = turned[0:4, 128:256]
+    table[24:32, :] = columns(jnp.where(pick < 4, pick, RX - 8 + pick))
+    copies = [pltpu.make_async_copy(table, out.at[d], sent.at[d]) for d in range(span_x)]
+    for copy in copies:
+        copy.start()
+    for copy in copies:
+        copy.wait()
 
 
 def block_edges(span_x, span_y, depth, lines, held):
@@ -388,8 +395,12 @@
             mark_shape(),
         ),
         in_specs=[vm()] * 3,
-        out_specs=(vm(),) * 2 + (hbm(),),
-        scratch_shapes=[pltpu.VMEM((16, GX), F32)],
+        out_specs=(hbm(), vm(), hbm()),
+        scratch_shapes=[
+            pltpu.VMEM((16, GX), F32),
+            pltpu.VMEM((32, EDGE), F32),
+            pltpu.SemaphoreType.DMA((span_x,)),
+        ],
         compiler_params=pltpu.CompilerParams(vmem_limit_bytes=12 * MIB),
         name="block_edges",
     )(depth, lines, held)
@@ -633,22 +644,20 @@
 
 
 def outgoing_body(
-    span_x, cap, slots, ids, pick, edges, n_x, n_y, inside, rim_x, rim_y, out, rows, _, pieces, q_x, q_y, source, counts
+    span_x, cap, slots, ids, pick, edges, n_x, n_y, inside, rim_x, rim_y, out, rows, _, pieces, q_x, q_y, source, counts, ready, sent
 ):
     blocks_x = KX * span_x
-    for d in range(span_x):
+    for d in range(span_x + 1):
         counts[d] = 0
     for d in range(span_x * cap):
         source[d] = 0
     for s in range(slots):
         held = jnp.maximum(ids[s], 0)
         owner = divide(held - blocks_x * divide(held, blocks_x), KX)
+        owner = jnp.where(ids[s] >= 0, owner, span_x)
         rank = counts[owner]
-
-        @pl.when(ids[s] >= 0)
-        def _():
-            source[owner * cap + jnp.minimum(rank, cap - 1)] = s
-            counts[owner] = rank + 1
+        source[owner * cap + jnp.minimum(rank, cap - 1)] = s
+        counts[owner] = rank + 1
 
     rows[...] = received_rows(span_x, cap, edges)
     near = jnp.dot(
@@ -702,6 +711,9 @@
                 pieces[start : start + 8, :] = strips[side][p][g]
     pieces[30 * STEP : 32 * STEP + 8, :] = jnp.zeros((2 * STEP + 8, 128), F32)
 
+    def put(r):
+        return pltpu.make_async_copy(ready.at[r], out.at[r], sent.at[r])
+
     tile_row = lax.broadcasted_iota(jnp.int32, (8, 128), 0)
     corner = (in_row >= 52) & (in_row < 60)
     for d in range(span_x):
@@ -721,8 +733,11 @@
             tail = jnp.where(tile_row >= 6, pltpu.roll(last(fold), 6, 0), tail)
             tail = jnp.where((tile_row == 3) & corner, pltpu.roll(last(fold_east), 8, 1), tail)
             tail = jnp.where((tile_row == 5) & corner, pltpu.roll(last(fold_west), 8, 1), tail)
-            out[d * cap + c, 0:24, :] = pieces[pl.ds(own, 24, stride=STEP), :]
-            out[d * cap + c, 24:32, :] = tail
+            ready[d * cap + c, 0:24, :] = pieces[pl.ds(own, 24, stride=STEP), :]
+            ready[d * cap + c, 24:32, :] = tail
+            put(d * cap + c).start()
+    for r in range(span_x * cap):
+        put(r).wait()
 
 
 def outgoing_blocks(span_x, cap, ids, pick, edges, rims, sums):
@@ -735,10 +750,11 @@
             mark_shape(),
         ),
         in_specs=[sm()] + [vm()] * 7,
-        out_specs=(vm(), vm(), hbm()),
+        out_specs=(hbm(), vm(), hbm()),
         scratch_shapes=[pltpu.VMEM((32 * STEP + 8, 128), F32)]
         + [pltpu.VMEM((SLOT_ROWS, 128), F32)] * 2
-        + [pltpu.SMEM((span_x * cap,), jnp.int32), pltpu.SMEM((span_x,), jnp.int32)],
+        + [pltpu.SMEM(((span_x + 1) * cap,), jnp.int32), pltpu.SMEM((span_x + 1,), jnp.int32)]
+        + [pltpu.VMEM((span_x * cap, 32, 128), F32), pltpu.SemaphoreType.DMA((span_x * cap,))],
         compiler_params=pltpu.CompilerParams(vmem_limit_bytes=12 * MIB),
         name="outgoing_blocks",
     )(ids, pick, edges, *rims, *sums)
@@ -1027,7 +1043,7 @@
     slots = tiles.shape[0]
     cap = (KX * KY + span_x - 1) // span_x
     both = ("gx", "gy")
-    bounds = [slots * i // 18 for i in (0, 12, 18)]
+    bounds = [slots * i // 18 for i in (0, 14, 18)]
 
     def solve(part, before, after):
         first, end = bounds[part], bounds[part + 1]

time: 71.3 us -> 71.4 us (level)
    all_to_all x1, waiting for transfers between devices: 4.35 us -> 3.11 us  [on_device(): got = lax.all_to_all(blocks, 'gx', split_axis=0, concat_axis=0, tiled=True)]
    all_to_all x1, waiting for transfers between devices: 3.68 us -> 4.9 us  [on_device(): sums = lax.all_to_all(dots, both, split_axis=0, concat_axis=0, tiled=True)]
  transfers between devices with their start and end apart: 4 -> 4, of which waited for: 3 -> 3; matrix products, arithmetic and copies ran while one was open for 0% -> 0% of each run, Pallas kernels for 32% -> 31%
where the time goes in v4:
time: 71.4 us; the launch traced here: 70.7 us
  Pallas kernels  30.9 us (43%)
  starting transfers between devices  16.9 us (24%)
  waiting for transfers between devices  11.3 us (16%)
  blocking collectives  6.66 us (9%)
  local copies, waits for them, and re-layouts  4.19 us (6%)
  between operations  0.72 us (1%)
    pallas_call x2, Pallas kernels, solve_columns(): pl.pallas_call(functools.partial(solve_body, first, count, extra), out_sh...  12.1 us
    pallas_call x1, Pallas kernels, face_sums(): pl.pallas_call(functools.partial(flux_body, slots, group), out_shape=(jax...  9.05 us
    all_to_all x1, blocking collectives, across(): return lax.all_to_all(lines, 'gy', split_axis=0, concat_axis=0, tiled=True)  6.66 us
    all_to_all x1, starting transfers between devices, on_device(): edges = lax.all_to_all(table, 'gx', split_axis=0, concat_axis=0, tiled=True)  6.3 us
    all_to_all x1, waiting for transfers between devices, on_device(): sums = lax.all_to_all(dots, both, split_axis=0, concat_axis=0, tiled=True)  4.9 us
    all_to_all x1, starting transfers between devices, across(): return lax.all_to_all(lines, 'gy', split_axis=0, concat_axis=0, tiled=True)  4.24 us
    unnamed x12, local copies, waits for them, and re-layouts  4.19 us
    all_to_all x1, starting transfers between devices, on_device(): got = lax.all_to_all(blocks, 'gx', split_axis=0, concat_axis=0, tiled=True)  3.65 us
  transfers between devices with their start and end apart: 4, of which 3 were waited for; matrix products, arithmetic and copies ran while one was open for 0% of the time, Pallas kernels for 31%

profile of v4, /device:TPU:0, one launch (start us, length us, event | category | flops | bytes accessed | tf_op | source)
XLA Modules:
  0.0 70.7 jit_solution(3748289899193502564)
XLA Ops:
  0.6 0.0 copy-start.2
  0.6 0.9 %copy-done.2 = s32[300,180]{0,1:T(8,128)S(1)} copy-done((s32[300,180]{0,1:T(8,128)S(1)}, s32[300,180]{0,1:T(8,128)}, u32[]{:S(2)}) %copy-start.2) | copy-done | bytes 216024
  1.6 0.8 %region_ends.1 = (f32[312,256]{1,0:T(8,128)S(1)}, f32[4,8,256]{2,1,0:T(8,128)}) custom-call(s32[180,300]{1,0:T(8,128)S(1)} %bitcast.10), custom_call_target="tpu_custom_call" | custom-call | tf_op jit(solution)/shard_map/region_ends/pallas_call | solution.py:421
  2.4 4.2 %all-to-all-start = ((f32[4,8,256]{2,1,0:T(8,128)}), f32[4,8,256]{2,1,0:T(8,128)S(1)}, u32[]{:S(2)}, u32[]{:S(2)}) async-start(f32[4,8,256]{2,1,0:T(8,128)} %get-tuple-element.42), calls=%async_computation | async-start | bytes 65536 | tf_op jit(solution)/shard_map/all_to_all | solution.py:1037
  6.6 0.0 copy-start
  6.6 1.0 %copy-done = s32[18,3000]{1,0:T(8,128)S(1)} copy-done((s32[18,3000]{1,0:T(8,128)S(1)}, s32[18,3000]{1,0:T(8,128)}, u32[]{:S(2)}) %copy-start) | copy-done | bytes 216024
  7.6 0.0 copy-start.1
  7.6 1.0 %copy-done.1 = f32[18,3000]{1,0:T(8,128)S(1)} copy-done((f32[18,3000]{1,0:T(8,128)S(1)}, f32[18,3000]{1,0:T(8,128)}, u32[]{:S(2)}) %copy-start.1) | copy-done | bytes 216024
  8.5 0.0 copy-start.3
  8.5 0.7 copy-done.3
  9.2 0.0 copy-start.5
  9.2 0.7 copy-done.5
  9.8 0.9 %column_tables.1 = (s32[608,128]{1,0:T(8,128)S(1)}, f32[608,128]{1,0:T(8,128)S(1)}, f32[720,128]{1,0:T(8,128)S(1)}, f32[96,256]{1,0:T(8,128)S(1)}, f32[24,128]{1...) custom-call(f32[29]{0:T(128)S(1)} %copy-done.5, s32[18]{0:T(128)S(1)} %copy-done.3, s32[18,3000]{1,0:T(8,128)S(1)} %copy-done, ...), custom_call_target="tpu_custom_call" | custom-call | flops 5000000 | bytes 3000000 | tf_op jit(solution)/shard_map/column_tables/pallas_call | solution.py:306
  10.7 0.0 all-to-all-done.lines
  10.7 1.1 %block_edges.1 = (f32[8,32,384]{2,1,0:T(8,128)}, f32[312,256]{1,0:T(8,128)S(1)}, f32[8,128]{1,0:T(8,128)S(1)}) custom-call(f32[312,256]{1,0:T(8,128)S(1)} %get-tuple-element.37.after.depth, f32[4,8,256]{2,1,0:T(8,128)S(1)} %all-to-all-done.lines, f32[8,128]{1,0:T(8,128)S(1)} %get-tuple-element.43.held), custom_call_target="tpu_custom_call" | custom-call | tf_op jit(solution)/shard_map/block_edges/pallas_call | solution.py:390
  11.8 6.3 %all-to-all-start.1 = ((f32[8,32,384]{2,1,0:T(8,128)}), f32[8,32,384]{2,1,0:T(8,128)S(1)}, u32[]{:S(2)}, u32[]{:S(2)}) async-start(f32[8,32,384]{2,1,0:T(8,128)} %get-tuple-element.44), calls=%async_computation.1 | async-start | bytes 786432 | tf_op jit(solution)/shard_map/all_to_all | solution.py:1058
  18.1 0.0 copy-start.4
  18.2 9.1 %face_sums.1 = (f32[656,128]{1,0:T(8,128)S(1)}, f32[18,32,128]{2,1,0:T(8,128)S(1)}, f32[18,32,128]{2,1,0:T(8,128)S(1)}) custom-call(f32[18,30,3000]{2,1,0:T(8,128)} %warm.5, f32[18,30,3000]{2,1,0:T(8,128)} %salt.5, s32[608,128]{1,0:T(8,128)S(1)} %get-tuple-element.38.n_rows, f32[608,128]{1,0:T(8,128)S(1)} %get-tuple-element.39.q_rows, ...), custom_call_target="tpu_custom_call" | custom-call | flops 40000000 | bytes 15000000 | tf_op jit(solution)/shard_map/face_sums/pallas_call | solution.py:589
  27.2 3.2 %all-to-all-done.1 = f32[8,32,384]{2,1,0:T(8,128)S(1)} async-done(((f32[8,32,384]{2,1,0:T(8,128)}), f32[8,32,384]{2,1,0:T(8,128)S(1)}, u32[]{:S(2)}, u32[]{:S(2)}) %all-to-all-start.1) | async-done | bytes 393248 | tf_op jit(solution)/shard_map/all_to_all | solution.py:1058
  30.5 0.0 copy-done.4
  30.5 2.3 %outgoing_blocks.1 = (f32[24,32,128]{2,1,0:T(8,128)}, s32[40,128]{1,0:T(8,128)S(1)}, f32[8,128]{1,0:T(8,128)S(1)}) custom-call(s32[18]{0:T(128)S(1)} %copy-done.4, f32[96,256]{1,0:T(8,128)S(1)} %get-tuple-element.41.pick, f32[256,384]{1,0:T(8,128)S(1)} %bitcast.6, f32[24,128]{1,0:T(8,128)S(1)} %get-tuple-element.45.n_x, ...), custom_call_target="tpu_custom_call" | custom-call | tf_op jit(solution)/shard_map/outgoing_blocks/pallas_call | solution.py:745
  32.7 3.6 %all-to-all-start.2 = ((f32[24,32,128]{2,1,0:T(8,128)}), f32[24,32,128]{2,1,0:T(8,128)S(1)}, u32[]{:S(2)}, u32[]{:S(2)}) async-start(f32[24,32,128]{2,1,0:T(8,128)} %get-tuple-element.55), calls=%async_computation.2 | async-start | bytes 786432 | tf_op jit(solution)/shard_map/all_to_all | solution.py:1062
  36.4 8.8 %column_solve.2 = (f32[18,30,3000]{2,1,0:T(8,128)}, f32[18,30,3000]{2,1,0:T(8,128)}, f32[8,128]{1,0:T(8,128)S(1)}) custom-call(f32[18,30,3000]{2,1,0:T(8,128)} %warm.5, f32[18,30,3000]{2,1,0:T(8,128)} %salt.5, s32[608,128]{1,0:T(8,128)S(1)} %get-tuple-element.38.n_rows, f32[608,128]{1,0:T(8,128)S(1)} %get-tuple-element.39.q_rows, ...), custom_call_target="tpu_custom_call" | custom-call | flops 28000000 | bytes 22400000 | tf_op jit(solution)/shard_map/column_solve/pallas_call | solution.py:212
  45.2 3.1 %all-to-all-done.2 = f32[24,32,128]{2,1,0:T(8,128)S(1)} async-done(((f32[24,32,128]{2,1,0:T(8,128)}), f32[24,32,128]{2,1,0:T(8,128)S(1)}, u32[]{:S(2)}, u32[]{:S(2)}) %all-to-all-start.2) | async-done | bytes 393248 | tf_op jit(solution)/shard_map/all_to_all | solution.py:1062
  48.3 1.4 %region_sums.1 = (f32[624,128]{1,0:T(8,128)S(1)}, f32[4,8,256]{2,1,0:T(8,128)S(1)}, f32[8,256]{1,0:T(8,128)S(1)}) custom-call(s32[40,128]{1,0:T(8,128)S(1)} %get-tuple-element.54.rows, f32[768,128]{1,0:T(8,128)S(1)} %bitcast.8, f32[8,128]{1,0:T(8,128)S(1)} %get-tuple-element.56.after), custom_call_target="tpu_custom_call" | custom-call | tf_op jit(solution)/shard_map/region_sums/pallas_call | solution.py:853
  49.7 6.7 %all_to_all.25.lines = f32[4,8,256]{2,1,0:T(8,128)S(1)} all-to-all(f32[4,8,256]{2,1,0:T(8,128)S(1)} %get-tuple-element.58), channel_id=1, replica_groups=mesh['gx'=8,'gy'=4] {'gy'}, dimensions={0} | all-to-all | bytes 65536 | tf_op jit(solution)/shard_map/all_to_all | solution.py:1037
  56.3 2.2 %krylov_basis.1 = (f32[4,312,256]{2,1,0:T(8,128)S(1)}, f32[312,256]{1,0:T(8,128)S(1)}, f32[32,8,128]{2,1,0:T(8,128)}, f32[8,128]{1,0:T(8,128)S(1)}) custom-call(f32[624,128]{1,0:T(8,128)S(1)} %get-tuple-element.57.region, f32[4,8,256]{2,1,0:T(8,128)S(1)} %all_to_all.25.lines, f32[8,256]{1,0:T(8,128)S(1)} %get-tuple-element.59.folded, ...), custom_call_target="tpu_custom_call" | custom-call | tf_op jit(solution)/shard_map/krylov_basis/pallas_call | solution.py:949
  58.5 2.7 %all-to-all-start.4 = ((f32[32,8,128]{2,1,0:T(8,128)}), f32[32,8,128]{2,1,0:T(8,128)S(1)}, u32[]{:S(2)}, u32[]{:S(2)}) async-start(f32[32,8,128]{2,1,0:T(8,128)} %get-tuple-element.64), calls=%async_computation.4 | async-start | bytes 262144 | tf_op jit(solution)/shard_map/all_to_all | solution.py:1069
  61.2 3.3 %column_solve.3 = (f32[18,30,3000]{2,1,0:T(8,128)}, f32[18,30,3000]{2,1,0:T(8,128)}, f32[8,128]{1,0:T(8,128)S(1)}) custom-call(f32[18,30,3000]{2,1,0:T(8,128)} %warm.5, f32[18,30,3000]{2,1,0:T(8,128)} %salt.5, s32[608,128]{1,0:T(8,128)S(1)} %get-tuple-element.38.n_rows, ...), custom_call_target="tpu_custom_call", output_to_operand_aliasing={{0}: (5, {}), {1}: (6, {})} | custom-call | flops 8000000 | bytes 6400000 | tf_op jit(solution)/shard_map/column_solve/pallas_call | solution.py:212
  64.6 4.9 %all-to-all-done.4 = f32[32,8,128]{2,1,0:T(8,128)S(1)} async-done(((f32[32,8,128]{2,1,0:T(8,128)}), f32[32,8,128]{2,1,0:T(8,128)S(1)}, u32[]{:S(2)}, u32[]{:S(2)}) %all-to-all-start.4) | async-done | bytes 131104 | tf_op jit(solution)/shard_map/all_to_all | solution.py:1069
  69.5 1.2 %combine.1 = (f32[180,300]{1,0:T(8,128)}, f32[180,300]{1,0:T(8,128)}) custom-call(f32[256,128]{1,0:T(8,128)S(1)} %bitcast.9, f32[4,312,256]{2,1,0:T(8,128)S(1)} %get-tuple-element.65.basis, f32[312,256]{1,0:T(8,128)S(1)} %get-tuple-element.66.diagonal, f32[8,128]{1,0:T(8,128)S(1)} %get-tuple-element.67.after), custom_call_target="tpu_custom_call" | custom-call | tf_op jit(solution)/shard_map/combine/pallas_call | solution.py:1026
Async XLA Ops:
  0.6 1.0 %copy-start.2 = (s32[300,180]{0,1:T(8,128)S(1)}, s32[300,180]{0,1:T(8,128)}, u32[]{:S(2)}) copy-start(s32[300,180]{0,1:T(8,128)} %param.13) | copy-start | bytes 648004
  2.4 8.4 %all-to-all-start = ((f32[4,8,256]{2,1,0:T(8,128)}), f32[4,8,256]{2,1,0:T(8,128)S(1)}, u32[]{:S(2)}, u32[]{:S(2)}) async-start(f32[4,8,256]{2,1,0:T(8,128)} %get-tuple-element.42), calls=%async_computation | async-start | bytes 65536 | tf_op jit(solution)/shard_map/all_to_all | solution.py:1037
  6.6 1.0 %copy-start = (s32[18,3000]{1,0:T(8,128)S(1)}, s32[18,3000]{1,0:T(8,128)}, u32[]{:S(2)}) copy-start(s32[18,3000]{1,0:T(8,128)} %depth.1) | copy-start | bytes 648004
  7.6 1.0 %copy-start.1 = (f32[18,3000]{1,0:T(8,128)S(1)}, f32[18,3000]{1,0:T(8,128)}, u32[]{:S(2)}) copy-start(f32[18,3000]{1,0:T(8,128)} %inflow.1) | copy-start | bytes 648004
  8.5 0.7 copy-start.3
  9.2 0.7 copy-start.5
  11.8 18.6 %all-to-all-start.1 = ((f32[8,32,384]{2,1,0:T(8,128)}), f32[8,32,384]{2,1,0:T(8,128)S(1)}, u32[]{:S(2)}, u32[]{:S(2)}) async-start(f32[8,32,384]{2,1,0:T(8,128)} %get-tuple-element.44), calls=%async_computation.1 | async-start | bytes 786432 | tf_op jit(solution)/shard_map/all_to_all | solution.py:1058
  18.1 12.3 %copy-start.4 = (s32[18]{0:T(128)S(1)}, s32[18]{0:T(128)}, u32[]{:S(2)}) copy-start(s32[18]{0:T(128)} %ids.3) | copy-start | bytes 220
  32.7 15.5 %all-to-all-start.2 = ((f32[24,32,128]{2,1,0:T(8,128)}), f32[24,32,128]{2,1,0:T(8,128)S(1)}, u32[]{:S(2)}, u32[]{:S(2)}) async-start(f32[24,32,128]{2,1,0:T(8,128)} %get-tuple-element.55), calls=%async_computation.2 | async-start | bytes 786432 | tf_op jit(solution)/shard_map/all_to_all | solution.py:1062
  58.5 11.0 %all-to-all-start.4 = ((f32[32,8,128]{2,1,0:T(8,128)}), f32[32,8,128]{2,1,0:T(8,128)S(1)}, u32[]{:S(2)}, u32[]{:S(2)}) async-start(f32[32,8,128]{2,1,0:T(8,128)} %get-tuple-element.64), calls=%async_computation.4 | async-start | bytes 262144 | tf_op jit(solution)/shard_map/all_to_all | solution.py:1069
